TPU v7x, 256 devices: a whole 4x4x8 slice. The times are simulated.
256 devices in a mesh: dp: 64 (over z, y, core), tensor: 4 (over x).
Axes of the slice: x: 4, y: 4, z: 8, core: 2. Of those that a mesh axis runs over, the one named last changes fastest.
Arguments:
- t_query: bfloat16 [49152, 5120], P('dp', 'tensor'), may hold values from -64 to 64
- t_key: bfloat16 [49152, 5120], P('dp', 'tensor'), may hold values from -64 to 64
- t_value: bfloat16 [49152, 5120], P('dp', 'tensor'), may hold values from -6 to 6
- t_segments: int32 [64, 768], P('dp'), may hold values from 0 to 23, never falling along the last dimension, each value on 1 to 384 neighbouring positions
- teacher_map: bfloat16 [5120, 1280], P('tensor'), may hold values from -0.625 to 0.625
- send_owner: int32 [49152], P(('dp', 'tensor')), may hold values from 0 to 63, as said below
- send_slot: int32 [49152], P(('dp', 'tensor')), may hold values from 0 to 191, as said below
- s_query: bfloat16 [49152, 1280], P(('dp', 'tensor')), may hold values from -64 to 64
- s_key: bfloat16 [49152, 1280], P(('dp', 'tensor')), may hold values from -64 to 64
- s_value: bfloat16 [49152, 1280], P(('dp', 'tensor')), may hold values from -6 to 6
- s_segments: int32 [256, 192], P(('dp', 'tensor')), may hold values from 0 to 23, never falling along the last dimension, each value on 1 to 96 neighbouring positions
- s_weight: bfloat16 [1280, 1280], P('dp'), may hold values from -0.625 to 0.625
Outputs:
- grad_context: float32 [49152, 1280], P(('dp', 'tensor'))
- grad_weight: float32 [1280, 1280], P('dp')
Inputs may be any that keep to these rules, and one draw needn't show every extreme that they name: `send_owner`: the rows of one device (aligned blocks of 192 rows) send at most 6 rows to one owner, and exactly 6 to some owner. Among rows with the same t = (j // 192) % 4, the pairs (send_owner, send_slot) are all different, so each owner receives exactly 192 rows of each t.
All inputs are finite; a program needn't handle non-finite values.
Results may differ from a plain program's by a relative error of at most 0.01.
Values may be sent and summed in bfloat16 or wider, within the bound.
No kernel may reach another device: no remote copies, remote signals or barrier semaphores. Data moves between devices by JAX's collectives and lax.ppermute only.
A program may use at most 128 MiB of HBM per device.

v0:
```python
import math

import jax
import jax.numpy as jnp
from jax import lax
from jax.sharding import PartitionSpec as P

HDT = 128
HDS = 64


def attend(query, keys, values, query_ids, key_ids, head_size):
    rows = query.shape[0]
    heads = query.shape[1] // head_size
    q_heads = query.reshape(rows, heads, head_size)
    k_heads = keys.reshape(-1, heads, head_size)
    v_heads = values.reshape(-1, heads, head_size)
    scores = jnp.einsum("qhd,khd->hqk", q_heads, k_heads, preferred_element_type=jnp.float32) * (
        1.0 / math.sqrt(head_size)
    )
    same = query_ids[:, None] == key_ids[None, :]
    scores = jnp.where(same[None], scores, jnp.float32(-1e30))
    top = jnp.max(scores, axis=2, keepdims=True)
    probs = jnp.exp(scores - top)
    weights = (probs / jnp.sum(probs, axis=2, keepdims=True)).astype(jnp.bfloat16)
    mixed = jnp.einsum("hqk,khd->qhd", weights, v_heads, preferred_element_type=jnp.float32)
    return mixed.reshape(rows, heads * head_size).astype(jnp.bfloat16)


def local(
    t_query,
    t_key,
    t_value,
    t_segments,
    teacher_map,
    send_owner,
    send_slot,
    s_query,
    s_key,
    s_value,
    s_segments,
    s_weight,
):
    group_ids = t_segments[0]
    rows = send_owner.shape[0]
    width = s_weight.shape[1]
    context = attend(t_query, t_key, t_value, group_ids, group_ids, HDT)
    target_rows = lax.psum_scatter(
        jnp.dot(context, teacher_map, preferred_element_type=jnp.float32),
        "tensor",
        scatter_dimension=0,
        tiled=True,
    ).astype(jnp.bfloat16)
    owners = lax.axis_size("dp")
    capacity = 2 * rows // owners
    position = jnp.arange(rows)
    same_owner = send_owner[:, None] == send_owner[None, :]
    earlier = position[:, None] > position[None, :]
    place = jnp.sum(jnp.logical_and(same_owner, earlier).astype(jnp.int32), axis=1)
    target_index = send_owner * capacity + place
    select = jnp.arange(owners * capacity)[:, None] == target_index[None, :]
    outgoing = jnp.dot(select.astype(jnp.bfloat16), target_rows, preferred_element_type=jnp.float32)
    outgoing = outgoing.astype(jnp.bfloat16).reshape(owners, capacity, width)
    slot_table = jnp.sum(jnp.where(select, send_slot[None, :] + 1, 0), axis=1) - 1
    slot_table = slot_table.reshape(owners, capacity)
    arrived, arrived_slots = (
        lax.all_to_all(outgoing, "dp", split_axis=0, concat_axis=0, tiled=True),
        lax.all_to_all(slot_table, "dp", split_axis=0, concat_axis=0, tiled=True),
    )
    landing = (position[:, None] == arrived_slots.reshape(1, owners * capacity)).astype(
        jnp.bfloat16
    )
    student_target = jnp.dot(
        landing, arrived.reshape(owners * capacity, width), preferred_element_type=jnp.float32
    )
    block_ids = s_segments[0]
    context = attend(s_query, s_key, s_value, block_ids, block_ids, HDS)
    weight = lax.all_gather(s_weight, "dp", axis=0, tiled=True)
    prediction = jnp.dot(context, weight, preferred_element_type=jnp.float32)
    error = (prediction - student_target).astype(jnp.bfloat16)
    grad_context = lax.dot_general(
        error, weight, (((1,), (1,)), ((), ())), preferred_element_type=jnp.float32
    )
    total_rows = rows * lax.axis_size("dp") * lax.axis_size("tensor")
    term = lax.dot_general(
        context, error, (((0,), (0,)), ((), ())), preferred_element_type=jnp.float32
    )
    whole = lax.psum(term.astype(jnp.bfloat16), "tensor").astype(jnp.float32)
    summed = lax.psum_scatter(whole, "dp", scatter_dimension=0, tiled=True)
    grad_weight = summed / math.sqrt(total_rows)
    return (grad_context, grad_weight)


def solution(mesh):
    placed = (
        P("dp", "tensor"),
        P("dp", "tensor"),
        P("dp", "tensor"),
        P("dp", None),
        P("tensor", None),
        P(("dp", "tensor")),
        P(("dp", "tensor")),
        P(("dp", "tensor"), None),
        P(("dp", "tensor"), None),
        P(("dp", "tensor"), None),
        P(("dp", "tensor"), None),
        P("dp", None),
    )
    return jax.shard_map(
        local,
        mesh=mesh,
        in_specs=placed,
        out_specs=(P(("dp", "tensor"), None), P("dp", None)),
        check_vma=False,
    )
```

profile of v0, /device:TPU:2, one launch (start us, length us, event | category | flops | bytes accessed | tf_op | source)
XLA Modules:
  0.0 548.6 jit_solution(898931803013282634)
XLA Ops:
  8.1 4.2 copy.48
  12.2 4.0 copy.49
  16.3 1.2 broadcast_compare_fusion
  17.5 4.0 copy.52
  21.5 14.6 %fusion.28 = (f32[10,768]{1,0:T(8,128)S(1)}, f32[10,768,768]{1,2,0:T(8,128)}) fusion(pred[768,768]{0,1:T(8,128)(4,1)} %broadcast_compare_fusion, bf16[768,10,128]{0,2,1:T(8,128)(2,1)} %bitcast.37, bf16[768,10,128]{0,2,1:T(8,128)(2,1)} %bitcast.38), kind=kOutput, calls=%fused_computation.46 | convolution fusion | flops 1533543168 | bytes 28145664 | tf_op jit(solution)/shard_map/sub | solution.py:24
  36.0 10.0 %fusion.15 = bf16[10,768,128]{1,2,0:T(8,128)(2,1)S(1)} fusion(bf16[768,10,128]{0,2,1:T(8,128)(2,1)} %bitcast.39, f32[10,768,768]{1,2,0:T(8,128)} %get-tuple-element.5, f32[10,768]{1,0:T(8,128)S(1)} %get-tuple-element.4), kind=kOutput, calls=%fused_computation.23 | convolution fusion | flops 1522728960 | bytes 27555840 | tf_op jit(solution)/shard_map/hqk,khd->qhd/dot_general | solution.py:26
  46.1 4.7 fusion.30
  51.8 0.8 sub.28
  52.6 12.3 %all-to-all-start = ((s32[64,1,6]{2,1,0:T(1,128)}), s32[64,1,6]{2,1,0:T(1,128)S(1)}, u32[]{:S(2)}, u32[]{:S(2)}) async-start(s32[64,1,6]{2,1,0:T(1,128)} %bitcast.7), calls=%async_computation | async-start | bytes 65536 | tf_op jit(solution)/shard_map/all_to_all | solution.py:68
  64.8 35.0 %reduce-scatter.2.cloned.1.call-done = f32[192,1280]{1,0:T(8,128)} async-done(((f32[768,1280]{1,0:T(8,128)}), f32[192,1280]{1,0:T(8,128)}) %reduce-scatter.2.cloned.1.call-update) | async-done | bytes 983056 | tf_op jit(solution)/shard_map/reduce_scatter | solution.py:48
  99.9 2.7 convolution_convert_fusion.1
  102.6 2.3 reshape.126
  104.8 10.8 %all-to-all-start.1 = ((bf16[64,6,1280]{2,1,0:T(8,128)(2,1)}), bf16[64,6,1280]{2,1,0:T(8,128)(2,1)}, u32[]{:S(2)}, u32[]{:S(2)}) async-start(bf16[64,6,1280]{2,1,0:T(8,128)(2,1)} %reshape.126), calls=%async_computation.2 | async-start | bytes 2621440 | tf_op jit(solution)/shard_map/all_to_all | solution.py:67
  115.7 2.1 copy.43
  117.9 2.1 copy.44
  120.0 2.1 copy.45
  122.2 4.7 fusion.27
  127.0 3.7 fusion.16
  131.2 0.7 reduce.4
  132.0 11.0 %all-gather.3.cloned.1.call-done = bf16[64,20,1280]{2,1,0:T(8,128)(2,1)} async-done(((bf16[1,20,1280]{2,1,0:T(8,128)(2,1)}), bf16[64,20,1280]{2,1,0:T(8,128)(2,1)}) %all-gather.3.cloned.1.call-update) | async-done | bytes 3276816 | tf_op jit(solution)/shard_map/all_gather | solution.py:78
  143.1 6.1 %reshape.129 = bf16[1280,1280]{1,0:T(8,128)(2,1)} reshape(bf16[64,20,1280]{2,1,0:T(8,128)(2,1)} %all-gather.3.cloned.1.call-done) | data formatting | bytes 6553600
  149.2 3.9 fusion.29
  153.6 2.2 reshape.127
  155.8 1.9 fusion.10
  157.7 0.8 copy-done.1
  158.5 3.8 convolution_convert_fusion
  162.3 0.6 copy-done.6
  163.0 0.6 dynamic-slice
  164.2 4.3 fusion.31
  168.5 74.0 %all-reduce.4.cloned.1.call-done = bf16[1280,1280]{1,0:T(8,128)(2,1)} async-done(((bf16[1280,1280]{1,0:T(8,128)(2,1)}), bf16[1280,1280]{1,0:T(8,128)(2,1)}) %all-reduce.4.cloned.1.call-update) | async-done | bytes 3276816 | tf_op jit(solution)/shard_map/psum | solution.py:88
  242.5 297.1 %all-reduce.5 = f32[1280,1280]{1,0:T(8,128)} all-reduce(bf16[1280,1280]{1,0:T(8,128)(2,1)} %all-reduce.4.cloned.1.call-done), channel_id=3, replica_groups=mesh['dp'=64,'tensor'=4] {'dp'}, use_global_device_ids=true, to_apply=%region_8.9.clone | all-reduce | flops 1638400 | bytes 9830400
  539.6 1.6 dynamic-slice_multiply_fusion
  (29 shorter events, 2.3 us)
Async XLA Ops:
  8.0 38.1 %copy-start = (bf16[1280,1280]{1,0:T(8,128)(2,1)S(1)}, bf16[1280,1280]{1,0:T(8,128)(2,1)}, u32[]{:S(2)}) copy-start(bf16[1280,1280]{1,0:T(8,128)(2,1)} %param.16) | copy-start | bytes 9830404
  8.0 8.2 %copy-start.4 = (s32[1,768]{1,0:T(1,128)S(1)}, s32[1,768]{1,0:T(1,128)}, u32[]{:S(2)}) copy-start(s32[1,768]{1,0:T(1,128)} %param.15) | copy-start | bytes 9220
  8.0 91.8 %reduce-scatter.2.cloned.1.call-start = ((), (), s32[]{:S(2)}) async-start(), calls=%async_computation.3 | async-start | bytes 4915200 | tf_op jit(solution)/shard_map/reduce_scatter | solution.py:48
  50.8 0.7 copy-start.2
  50.8 0.9 copy-start.5
  50.8 92.3 %all-gather.3.cloned.1.call-start = ((), (), s32[]{:S(2)}) async-start(), calls=%async_computation.5 | async-start | bytes 3993600 | tf_op jit(solution)/shard_map/all_gather | solution.py:78
  52.6 52.3 %all-to-all-start = ((s32[64,1,6]{2,1,0:T(1,128)}), s32[64,1,6]{2,1,0:T(1,128)S(1)}, u32[]{:S(2)}, u32[]{:S(2)}) async-start(s32[64,1,6]{2,1,0:T(1,128)} %bitcast.7), calls=%async_computation | async-start | bytes 65536 | tf_op jit(solution)/shard_map/all_to_all | solution.py:68
  104.8 17.3 %copy-start.3 = (s32[1,192]{1,0:T(1,128)S(1)}, s32[1,192]{1,0:T(1,128)}, u32[]{:S(2)}) copy-start(s32[1,192]{1,0:T(1,128)} %param.22) | copy-start | bytes 2308
  104.8 48.7 %all-to-all-start.1 = ((bf16[64,6,1280]{2,1,0:T(8,128)(2,1)}), bf16[64,6,1280]{2,1,0:T(8,128)(2,1)}, u32[]{:S(2)}, u32[]{:S(2)}) async-start(bf16[64,6,1280]{2,1,0:T(8,128)(2,1)} %reshape.126), calls=%async_computation.2 | async-start | bytes 2621440 | tf_op jit(solution)/shard_map/all_to_all | solution.py:67
  115.7 126.8 %all-reduce.4.cloned.1.call-start = ((), (), s32[]{:S(2)}) async-start(), calls=%async_computation.4 | async-start | bytes 6553600 | tf_op jit(solution)/shard_map/psum | solution.py:88
  157.7 0.8 copy-start.1
  162.3 0.7 copy-start.6
Sparse Core Ops, SparseCore 0:
  50.9 48.9 reduce-scatter.1
  162.4 80.0 all-reduce.3
Sparse Core Ops, SparseCore 1:
  53.9 89.1 all-gather.2
where the time goes:
time: 550 us; the launch traced here: 549 us
  blocking collectives  297 us (54%)
  waiting for transfers between devices  121 us (22%)
  matrix products  54.3 us (10%)
  local copies, waits for them, and re-layouts  32.6 us (6%)
  starting transfers between devices  23.3 us (4%)
  between operations  16.3 us (3%)
    unnamed x1, blocking collectives  297 us
    psum x1, waiting for transfers between devices, local(): whole = lax.psum(term.astype(jnp.bfloat16), 'tensor').astype(jnp.float32)  74 us
    reduce_scatter x1, waiting for transfers between devices, local(): lax.psum_scatter(jnp.dot(context, teacher_map, preferred_element_type=jnp...  35 us
    unnamed x22, local copies, waits for them, and re-layouts  26.7 us
    sub x2, matrix products, attend(): probs = jnp.exp(scores - top)  19.3 us
    dot_general x2, matrix products, attend(): jnp.einsum('hqk,khd->qhd', weights, v_heads, preferred_element_type=jnp.f...  13.7 us
    all_to_all x1, starting transfers between devices, local(): lax.all_to_all(slot_table, 'dp', split_axis=0, concat_axis=0, tiled=True)  12.3 us
    all_gather x1, waiting for transfers between devices, local(): weight = lax.all_gather(s_weight, 'dp', axis=0, tiled=True)  11 us
  transfers between devices with their start and end apart: 5, of which 4 were waited for; matrix products, arithmetic and copies ran while one was open for 7% of the time, Pallas kernels for 0%

commit v1 on v0

v1 whole, which is shorter than its diff:
```python
import functools
import math

import jax
import jax.numpy as jnp
import numpy as np
from jax import lax
from jax.experimental import pallas as pl
from jax.experimental.pallas import tpu as pltpu
from jax.sharding import Mesh, PartitionSpec as P

HDT = 128
HDS = 64
LOG2E = 1.4426950408889634
BIG = 1e30
BF = jnp.bfloat16
F32 = jnp.float32
DP = ("z", "y", "core")
NT = (((1,), (1,)), ((), ()))
TN = (((0,), (0,)), ((), ()))
WIDE = 384
VMEM_LIMIT = 56 * 1024 * 1024


def ring(n, k):
    return [(i, (i + k) % n) for i in range(n)]


def params():
    return pltpu.CompilerParams(vmem_limit_bytes=VMEM_LIMIT)


def segment_columns(ids):
    n = ids.shape[1]
    lane = lax.broadcasted_iota(jnp.int32, (128, n), 0)
    hot = jnp.transpose((lane == ids).astype(F32))
    return hot.astype(BF), ((hot - 1.0) * BIG).astype(BF)


def softmax_rows(scores, scale):
    top = jnp.max(scores, axis=1, keepdims=True)
    return jnp.exp2((scores - top) * scale).astype(BF)


def teacher_kernel(x_ref, ids_ref, q_ref, k_ref, v_ref, map_ref, own_ref, right_ref, up_ref, down_ref, left_ref,
                   qx, kx, ve, ctx, packed):
    step = pl.program_id(0)
    rows = ctx.shape[0]
    half = rows // 2
    scale = LOG2E / math.sqrt(HDT)

    @pl.when(step == 0)
    def _():
        hot, far = segment_columns(ids_ref[...])
        qx[...] = hot
        kx[...] = far
        ve[:, HDT:] = jnp.ones((rows, HDT), BF)

    for h in range(2):
        cols = slice(h * HDT, (h + 1) * HDT)
        ke = jnp.concatenate([k_ref[:, cols], kx[...]], axis=1)
        ve[:, :HDT] = v_ref[:, cols]
        for r in range(0, rows, 256):
            qe = jnp.concatenate([q_ref[r:r + 256, cols], qx[r:r + 256, :]], axis=1)
            s = lax.dot_general(qe, ke, NT, preferred_element_type=F32)
            p = softmax_rows(s, scale)
            o = jnp.dot(p, ve[...], preferred_element_type=F32)
            c = (o[:, :HDT] / o[:, HDT:]).astype(BF)
            ctx[r:r + 256, pl.ds(pl.multiple_of(step * 256 + h * HDT, HDT), HDT)] = c

    @pl.when(step == pl.num_programs(0) - 1)
    def _():
        block = map_ref.shape[1] // 4
        for r in range(0, half, 192):
            a = jnp.dot(ctx[r:r + 192, :], map_ref[...], preferred_element_type=F32)
            b = jnp.dot(ctx[half + r:half + r + 192, :], map_ref[...], preferred_element_type=F32)
            for n in range(4):
                packed[n, r:r + 192, :] = jnp.concatenate(
                    [a[:, n * block:(n + 1) * block], b[:, n * block:(n + 1) * block]], axis=1
                ).astype(BF)
        x = x_ref[0]
        own_ref[...] = packed[x]
        right_ref[...] = packed[lax.rem(x + 1, 4)]
        far = lax.rem(x + 2, 4)
        up_ref[...] = packed[far, :half // 2, :]
        down_ref[...] = packed[far, half // 2:, :]
        left_ref[...] = packed[lax.rem(x + 3, 4)]


def teacher(x, ids, q, k, v, tmap):
    rows, width = q.shape
    out = tmap.shape[1]
    half = rows // 2
    wide = out // 2
    pair = 2 * HDT
    steps = width // pair
    s = lambda r: jax.ShapeDtypeStruct((r, wide), BF)
    whole = lambda r: pl.BlockSpec((r, wide), lambda i: (0, 0))
    return pl.pallas_call(
        teacher_kernel,
        grid=(steps,),
        in_specs=[
            pl.BlockSpec(memory_space=pltpu.SMEM),
            pl.BlockSpec((1, rows), lambda i: (0, 0)),
            pl.BlockSpec((rows, pair), lambda i: (0, i)),
            pl.BlockSpec((rows, pair), lambda i: (0, i)),
            pl.BlockSpec((rows, pair), lambda i: (0, i)),
            pl.BlockSpec((width, out), lambda i: (0, 0)),
        ],
        out_specs=[whole(half), whole(half), whole(half // 2), whole(half // 2), whole(half)],
        out_shape=[s(half), s(half), s(half // 2), s(half // 2), s(half)],
        scratch_shapes=[
            pltpu.VMEM((rows, 128), BF),
            pltpu.VMEM((rows, 128), BF),
            pltpu.VMEM((rows, pair), BF),
            pltpu.VMEM((rows, width), BF),
            pltpu.VMEM((4, half, wide), BF),
        ],
        compiler_params=params(),
        cost_estimate=pl.CostEstimate(flops=10 * 10**9, bytes_accessed=10 * 2**20, transcendentals=6 * 10**6),
        name="teacher",
    )(x, ids, q, k, v, tmap)


def student_kernel(ids_ref, q_ref, k_ref, v_ref, o_ref):
    rows, width = q_ref.shape
    scale = LOG2E / math.sqrt(HDS)
    hot, far = segment_columns(ids_ref[...])
    low = lax.broadcasted_iota(jnp.int32, (rows, 128), 1) < HDS
    ones = jnp.ones((rows, 128), BF)
    for g in range(0, width, 128):
        cols = slice(g, g + 128)
        ke = jnp.concatenate([k_ref[:, cols], far], axis=1)
        ve = jnp.concatenate([v_ref[:, cols], ones], axis=1)
        q = q_ref[:, cols]
        done = []
        for keep in (low, jnp.logical_not(low)):
            qe = jnp.concatenate([jnp.where(keep, q, jnp.zeros_like(q)), hot], axis=1)
            s = lax.dot_general(qe, ke, NT, preferred_element_type=F32)
            o = jnp.dot(softmax_rows(s, scale), ve, preferred_element_type=F32)
            done.append(o[:, :128] / o[:, 128:])
        o_ref[:, cols] = jnp.where(low, done[0], done[1]).astype(BF)


def student(ids, q, k, v):
    return pl.pallas_call(
        student_kernel,
        out_shape=jax.ShapeDtypeStruct(q.shape, BF),
        compiler_params=params(),
        cost_estimate=pl.CostEstimate(flops=10**9, bytes_accessed=2 * 2**20, transcendentals=10**6),
        name="student",
    )(ids, q, k, v)


def select_kernel(idx_ref, slot_ref, own_ref, a_ref, b_ref, o_ref, rows_ref):
    half, wide = own_ref.shape
    block = wide // 2
    total = (own_ref[...].astype(F32) + a_ref[...].astype(F32)) + b_ref[...].astype(F32)
    mark = jnp.transpose(jnp.broadcast_to(slot_ref[...].astype(F32) + 1.0, (128, 2 * half)))[:, :WIDE - block]
    rows_ref[:half, :] = jnp.concatenate([total[:, :block], mark[:half, :]], axis=1).astype(BF)
    rows_ref[half:, :] = jnp.concatenate([total[:, block:], mark[half:, :]], axis=1).astype(BF)
    idx = idx_ref[...]
    for r in range(0, o_ref.shape[0], 256):
        row = lax.broadcasted_iota(jnp.int32, (256, 2 * half), 0) + r
        hot = (row == idx).astype(F32).astype(BF)
        o_ref[r:r + 256, :] = jnp.dot(hot, rows_ref[...], preferred_element_type=F32).astype(BF)


def select(idx, slot, own, a, b, outgoing):
    rows = idx.shape[1]
    return pl.pallas_call(
        select_kernel,
        out_shape=jax.ShapeDtypeStruct((outgoing, WIDE), BF),
        scratch_shapes=[pltpu.VMEM((rows, WIDE), BF)],
        compiler_params=params(),
        cost_estimate=pl.CostEstimate(flops=10**9, bytes_accessed=4 * 2**20, transcendentals=0),
        name="pick",
    )(idx, slot, own, a, b)


def land_kernel(core_ref, base_ref, arrived_ref, pred_ref, ctxt_ref, err_ref, other_ref, own_ref):
    rows = err_ref.shape[0]
    block = WIDE - 64
    slot = jnp.transpose(arrived_ref[:, 256:].astype(F32))[64:65, :]
    dst = jnp.where(slot > 0.5, slot.astype(jnp.int32) + base_ref[...], -1)
    valid = lax.broadcasted_iota(jnp.int32, (256, WIDE), 1) < block
    for r in range(0, rows, 256):
        row = lax.broadcasted_iota(jnp.int32, (256, dst.shape[1]), 0) + r
        hot = (row == dst).astype(F32).astype(BF)
        target = jnp.dot(hot, arrived_ref[...], preferred_element_type=F32)
        err_ref[r:r + 256, :] = jnp.where(valid, pred_ref[r:r + 256, :] - target, 0.0).astype(BF)
    core = core_ref[0]
    other_ref[...] = jnp.dot(ctxt_ref[1 - core], err_ref[...], preferred_element_type=F32).astype(BF)
    own_ref[...] = jnp.dot(ctxt_ref[core], err_ref[...], preferred_element_type=F32)


def land(core, base, arrived, pred, ctxt):
    rows = pred.shape[0]
    out = ctxt.shape[1]
    vm = pl.BlockSpec(memory_space=pltpu.VMEM)
    return pl.pallas_call(
        land_kernel,
        in_specs=[pl.BlockSpec(memory_space=pltpu.SMEM), vm, vm, vm, vm],
        out_shape=[
            jax.ShapeDtypeStruct((rows, WIDE), BF),
            jax.ShapeDtypeStruct((out, WIDE), BF),
            jax.ShapeDtypeStruct((out, WIDE), F32),
        ],
        compiler_params=params(),
        cost_estimate=pl.CostEstimate(flops=2 * 10**9, bytes_accessed=8 * 2**20, transcendentals=0),
        name="land",
    )(core, base, arrived, pred, ctxt)


def grad_kernel(x_ref, err_ref, w_ref, own_ref, right_ref, up_ref, down_ref, left_ref):
    quarter = own_ref.shape[0]
    x = x_ref[0]

    def part(n):
        start = pl.multiple_of(lax.rem(x + n, 4) * quarter, quarter)
        return lax.dot_general(err_ref[pl.ds(start, quarter), :], w_ref[...], NT, preferred_element_type=F32)

    far = part(2).astype(BF)
    up_ref[...] = far[:quarter // 2, :]
    down_ref[...] = far[quarter // 2:, :]
    right_ref[...] = part(1).astype(BF)
    left_ref[...] = part(3).astype(BF)
    own_ref[...] = part(0)


def grad_parts(x, err, weight):
    quarter = err.shape[0] // 4
    width = weight.shape[0]
    vm = pl.BlockSpec(memory_space=pltpu.VMEM)
    s = lambda r, t=BF: jax.ShapeDtypeStruct((r, width), t)
    return pl.pallas_call(
        grad_kernel,
        in_specs=[pl.BlockSpec(memory_space=pltpu.SMEM), vm, vm],
        out_shape=[s(quarter, F32), s(quarter), s(quarter // 2), s(quarter // 2), s(quarter)],
        compiler_params=params(),
        cost_estimate=pl.CostEstimate(flops=10**9, bytes_accessed=4 * 2**20, transcendentals=0),
        name="grad",
    )(x, err, weight)


def relay_sum(right, up, down, left):
    n = up.shape[0]
    from_left = lax.ppermute(up, "tensor", ring(4, 1))
    from_right = lax.ppermute(down, "tensor", ring(4, 3))
    right = jnp.concatenate([(right[:n].astype(F32) + from_left.astype(F32)).astype(BF), right[n:]])
    left = jnp.concatenate([left[:n], (left[n:].astype(F32) + from_right.astype(F32)).astype(BF)])
    return lax.ppermute(right, "tensor", ring(4, 1)), lax.ppermute(left, "tensor", ring(4, 3))


def gather_x(a):
    x = lax.axis_index("tensor")
    parts = [a] + [lax.ppermute(a, "tensor", ring(4, k)) for k in (1, 2, 3)]
    whole = jnp.stack(parts)
    order = lax.rem(x - jnp.arange(4) + 4, 4)
    return jnp.take(whole, order, axis=0)


def local(
    t_query, t_key, t_value, t_segments, teacher_map, send_owner, send_slot, s_query, s_key, s_value, s_segments, s_weight
):
    x = lax.axis_index("tensor")
    core = lax.axis_index("core")
    rows = send_owner.shape[0]
    width = s_weight.shape[1]
    n_z, n_y, n_c = (lax.axis_size(a) for a in DP)
    owners = n_z * n_y * n_c
    capacity = 2 * rows // owners
    block = width // 4
    unit = 4 * capacity
    xs = x.astype(jnp.int32).reshape(1)
    cs = core.astype(jnp.int32).reshape(1)

    mine = lax.dynamic_slice(s_weight, (0, x * block), (s_weight.shape[0], block))
    own_rows = s_weight.shape[0]
    pad = -own_rows % 8
    mine = jnp.pad(mine, ((0, pad), (0, WIDE - block)))
    near = lax.all_to_all(
        jnp.broadcast_to(mine[None], (n_y * n_c,) + mine.shape), ("y", "core"), 0, 0, tiled=True
    ).reshape(n_y * n_c * mine.shape[0], WIDE)
    weight = lax.all_gather(near, "z", axis=0, tiled=True)
    weight = weight.reshape(owners, own_rows + pad, WIDE)[:, :own_rows].reshape(width, WIDE)

    position = jnp.arange(rows)
    same_owner = send_owner[:, None] == send_owner[None, :]
    earlier = position[:, None] > position[None, :]
    place = jnp.sum(jnp.logical_and(same_owner, earlier).astype(jnp.int32), axis=1)
    index = send_owner * unit + x * capacity + place
    table = jnp.stack([index, send_slot])
    tables = gather_x(table)
    index = tables[:, 0].reshape(1, 4 * rows)
    slots = tables[:, 1].reshape(1, 4 * rows)

    own, right, up, down, left = teacher(xs, t_segments, t_query, t_key, t_value, teacher_map)
    a, b = relay_sum(right, up, down, left)
    outgoing = select(index, slots, own, a, b, owners * unit)
    arrived = lax.all_to_all(outgoing, DP, 0, 0, tiled=True)

    context = student(s_segments, s_query, s_key, s_value)
    contexts = gather_x(context).reshape(4 * rows, width)
    prediction = jnp.dot(contexts, weight, preferred_element_type=F32)
    turned = contexts.T.reshape(n_z, n_y, n_c, own_rows, 4 * rows)
    turned = jnp.pad(jnp.transpose(turned, (2, 0, 1, 3, 4)), ((0, 0), (0, 0), (0, 0), (0, pad), (0, 0)))
    turned = turned.reshape(n_c, n_z * n_y * (own_rows + pad), 4 * rows)

    base = np.array([[(r % unit) // capacity * rows - 1 for r in range(owners * unit)]], np.int32)
    err, other, term = land(cs, jnp.asarray(base), arrived, prediction, turned)

    term = (term + lax.ppermute(other, "core", ring(2, 1)).astype(F32)).astype(BF)
    terms = lax.all_to_all(term, ("z", "y"), 0, 0, tiled=True)
    terms = terms.reshape(n_z * n_y, own_rows + pad, WIDE)[:, :own_rows, :block]
    summed = jnp.sum(terms.astype(F32), axis=0) * (1.0 / math.sqrt(4 * rows * owners))
    grad_weight = jnp.transpose(gather_x(summed), (1, 0, 2)).reshape(own_rows, width)

    own, right, up, down, left = grad_parts(xs, err, weight)
    a, b = relay_sum(right, up, down, left)
    grad_context = own + a.astype(F32) + b.astype(F32)
    return (grad_context, grad_weight)


def solution(mesh):
    fine = Mesh(mesh.devices.reshape(8, 4, 2, 4), DP + ("tensor",))
    both = DP + ("tensor",)
    placed = (
        P(DP, "tensor"),
        P(DP, "tensor"),
        P(DP, "tensor"),
        P(DP, None),
        P("tensor", None),
        P(both),
        P(both),
        P(both, None),
        P(both, None),
        P(both, None),
        P(both, None),
        P(DP, None),
    )
    return jax.shard_map(
        local, mesh=fine, in_specs=placed, out_specs=(P(both, None), P(DP, None)), check_vma=False
    )
```

time: 550 us -> 185 us (0.34)
  blocking collectives: 297 us -> 0 us
  waiting for transfers between devices: 121 us -> 40.2 us
  matrix products: 54.3 us -> 3.42 us
  Pallas kernels: 0 us -> 34.6 us
  starting transfers between devices: 23.3 us -> 53.1 us
  other arithmetic: 3.95 us -> 13.9 us
  local copies, waits for them, and re-layouts: 32.6 us -> 24.1 us
    unnamed x1 -> x0, blocking collectives: 297 us -> none
    psum x1 -> x0, waiting for transfers between devices: 74 us -> none  [local(): whole = lax.psum(term.astype(jnp.bfloat16), 'tensor').astype(jnp.float32)]
    reduce_scatter x1 -> x0, waiting for transfers between devices: 35 us -> none  [local(): lax.psum_scatter(jnp.dot(context, teacher_map, preferred_element_type=jnp...]
    pallas_call x0 -> x5, Pallas kernels: none -> 34.6 us  [the longest x1 16.5 us: teacher(): pl.pallas_call(teacher_kernel, grid=(steps,), in_specs=[pl.BlockSpec(memo...]
    dot_general x8 -> x1, matrix products: 35 us -> 3.42 us  [local(): prediction = jnp.dot(contexts, weight, preferred_element_type=F32)]
    ppermute x0 -> x18, starting transfers between devices: none -> 30.1 us  [the longest x9 16.5 us: gather_x(): parts = [a] + [lax.ppermute(a, 'tensor', ring(4, k)) for k in (1, 2, 3)]]
    unnamed x22 -> x23, local copies, waits for them, and re-layouts: 26.7 us -> 3.65 us
    sub x2 -> x0, matrix products: 19.3 us -> none  [attend(): probs = jnp.exp(scores - top)]
  transfers between devices with their start and end apart: 5 -> 22, of which waited for: 4 -> 9; matrix products, arithmetic and copies ran while one was open for 7% -> 20% of each run, Pallas kernels for 0% -> 16%
where the time goes in v1:
time: 185 us; the launch traced here: 184 us
  starting transfers between devices  53.1 us (29%)
  waiting for transfers between devices  40.2 us (22%)
  Pallas kernels  34.6 us (19%)
  local copies, waits for them, and re-layouts  24.1 us (13%)
  between operations  14.3 us (8%)
  other arithmetic  13.9 us (8%)
  matrix products  3.42 us (2%)
    pallas_call x1, Pallas kernels, teacher(): pl.pallas_call(teacher_kernel, grid=(steps,), in_specs=[pl.BlockSpec(memo...  16.5 us
    ppermute x9, starting transfers between devices, gather_x(): parts = [a] + [lax.ppermute(a, 'tensor', ring(4, k)) for k in (1, 2, 3)]  16.5 us
    all_gather x1, waiting for transfers between devices, local(): weight = lax.all_gather(near, 'z', axis=0, tiled=True)  14.9 us
    all_to_all x1, waiting for transfers between devices, local(): terms = lax.all_to_all(term, ('z', 'y'), 0, 0, tiled=True)  14.5 us
    all_to_all x1, starting transfers between devices, local(): arrived = lax.all_to_all(outgoing, DP, 0, 0, tiled=True)  12.2 us
    all_to_all x1, starting transfers between devices, local(): terms = lax.all_to_all(term, ('z', 'y'), 0, 0, tiled=True)  6.36 us
    ppermute x2, starting transfers between devices, relay_sum(): from_right = lax.ppermute(down, 'tensor', ring(4, 3))  6.33 us
    pallas_call x1, Pallas kernels, land(): pl.pallas_call(land_kernel, in_specs=[pl.BlockSpec(memory_space=pltpu.SME...  6.13 us
  transfers between devices with their start and end apart: 22, of which 9 were waited for; matrix products, arithmetic and copies ran while one was open for 20% of the time, Pallas kernels for 16%

profile of v1, /device:TPU:2, one launch (start us, length us, event | category | flops | bytes accessed | tf_op | source)
XLA Modules:
  0.0 183.7 jit_solution(15075644183172397927)
XLA Ops:
  9.5 2.1 %collective-permute-start.1 = (s32[2,192]{1,0:T(2,128)S(1)}, s32[2,192]{1,0:T(2,128)S(1)}, u32[]{:S(2)}, u32[]{:S(2)}) collective-permute-start(s32[2,192]{1,0:T(2,128)S(1)} %get-tuple-element.33), channel_id=1, source_target_pairs={{0,2},{1,3},{2,0},{3,1},{4,6},{5,7},{6,4},{7,5},{8,10},{9,11},{10,... | collective-permute-start | bytes 4616 | tf_op jit(solution)/shard_map/ppermute | solution.py:257
  11.6 1.6 collective-permute-start
  14.4 4.5 %all-to-all-start.1 = ((bf16[8,24,384]{2,1,0:T(8,128)(2,1)}), bf16[8,24,384]{2,1,0:T(8,128)(2,1)S(1)}, u32[]{:S(2)}, u32[]{:S(2)}) async-start(bf16[8,24,384]{2,1,0:T(8,128)(2,1)} %broadcast_in_dim.52), calls=%async_computation.1 | async-start | bytes 294912 | tf_op jit(solution)/shard_map/all_to_all | solution.py:282
  18.9 16.5 %teacher.1 = (bf16[384,640]{1,0:T(8,128)(2,1)}, bf16[384,640]{1,0:T(8,128)(2,1)}, bf16[192,640]{1,0:T(8,128)(2,1)}, bf16[192,640]{1,0:T(8,128)(2,1)}, bf16[384,640]{1,0:T(8,128)(2,1)}) custom-call(s32[1]{0:T(128)} %bitcast.x_ref, s32[1,768]{1,0:T(1,128)} %ids_ref.2, bf16[768,1280]{1,0:T(8,128)(2,1)} %q_ref.2, bf16[768,1280]{1,0:T(8,128)(2,1)} %k_ref.2, ...), custom_call_target="tpu_custom_call" | custom-call | flops 10000000000 | bytes 10485760 | tf_op jit(solution)/shard_map/teacher/pallas_call | solution.py:99
  36.0 2.2 %collective-permute-start.5 = (bf16[192,640]{1,0:T(8,128)(2,1)}, bf16[192,640]{1,0:T(8,128)(2,1)S(1)}, u32[]{:S(2)}, u32[]{:S(2)}) collective-permute-start(bf16[192,640]{1,0:T(8,128)(2,1)} %get-tuple-element.19), channel_id=1, source_target_pairs={{0,3},{1,0},{2,1},{3,2},{4,7},{5,4},{6,5},{7,6},{8,11},{9,8},{10,9... | collective-permute-start | bytes 737288 | tf_op jit(solution)/shard_map/ppermute | solution.py:249
  40.2 4.2 %collective-permute-done.5 = bf16[192,640]{1,0:T(8,128)(2,1)S(1)} collective-permute-done((bf16[192,640]{1,0:T(8,128)(2,1)}, bf16[192,640]{1,0:T(8,128)(2,1)S(1)}, u32[]{:S(2)}, u32[]{:S(2)}) %collective-permute-start.5) | collective-permute-done | bytes 245792 | tf_op jit(solution)/shard_map/ppermute | solution.py:249
  45.4 2.9 %collective-permute-start.6 = (bf16[384,640]{1,0:T(8,128)(2,1)S(1)}, bf16[384,640]{1,0:T(8,128)(2,1)S(1)}, u32[]{:S(2)}, u32[]{:S(2)}) collective-permute-start(bf16[384,640]{1,0:T(8,128)(2,1)S(1)} %pad_maximum_fusion.2), channel_id=1, source_target_pairs={{0,3},{1,0},{2,1},{3,2},{4,7},{5,4},{6,5},{7,6},{8,11},{9,8},{10,9... | collective-permute-start | bytes 1474568 | tf_op jit(solution)/shard_map/ppermute | solution.py:252
  48.6 3.8 %student.1 = bf16[192,1280]{1,0:T(8,128)(2,1)} custom-call(s32[1,192]{1,0:T(1,128)} %ids_ref.3, bf16[192,1280]{1,0:T(8,128)(2,1)} %q_ref.3, bf16[192,1280]{1,0:T(8,128)(2,1)} %k_ref.3, bf16[192,1280]{1,0:T(8,128)(2,1)} %v_ref.3), custom_call_target="tpu_custom_call" | custom-call | flops 1000000000 | bytes 2097152 | tf_op jit(solution)/shard_map/student/pallas_call | solution.py:146
  52.5 3.5 %collective-permute-start.9 = (bf16[192,1280]{1,0:T(8,128)(2,1)}, bf16[192,1280]{1,0:T(8,128)(2,1)S(1)}, u32[]{:S(2)}, u32[]{:S(2)}) collective-permute-start(bf16[192,1280]{1,0:T(8,128)(2,1)} %student.1), channel_id=1, source_target_pairs={{0,3},{1,0},{2,1},{3,2},{4,7},{5,4},{6,5},{7,6},{8,11},{9,8},{10,9... | collective-permute-start | bytes 1474568 | tf_op jit(solution)/shard_map/ppermute | solution.py:257
  56.0 2.1 %collective-permute-start.8 = (bf16[192,1280]{1,0:T(8,128)(2,1)}, bf16[192,1280]{1,0:T(8,128)(2,1)S(1)}, u32[]{:S(2)}, u32[]{:S(2)}) collective-permute-start(bf16[192,1280]{1,0:T(8,128)(2,1)} %student.1), channel_id=1, source_target_pairs={{0,2},{1,3},{2,0},{3,1},{4,6},{5,7},{6,4},{7,5},{8,10},{9,11},{10,... | collective-permute-start | bytes 1474568 | tf_op jit(solution)/shard_map/ppermute | solution.py:257
  58.2 2.5 %collective-permute-start.7 = (bf16[192,1280]{1,0:T(8,128)(2,1)}, bf16[192,1280]{1,0:T(8,128)(2,1)S(1)}, u32[]{:S(2)}, u32[]{:S(2)}) collective-permute-start(bf16[192,1280]{1,0:T(8,128)(2,1)} %student.1), channel_id=1, source_target_pairs={{0,1},{1,2},{2,3},{3,0},{4,5},{5,6},{6,7},{7,4},{8,9},{9,10},{10,1... | collective-permute-start | bytes 1474568 | tf_op jit(solution)/shard_map/ppermute | solution.py:257
  64.4 4.1 %pick.1 = bf16[1536,384]{1,0:T(8,128)(2,1)} custom-call(s32[1,768]{1,0:T(1,128)} %reshape_squeeze.6.idx_ref, s32[1,768]{1,0:T(1,128)} %reshape_squeeze.7.slot_ref, bf16[384,640]{1,0:T(8,128)(2,1)} %get-tuple-element.15.own_ref, bf16[384,640]{1,0:T(8,128)(2,1)} %collective-permute-done.4.a_ref, bf16[384,640]{1,0:T(8,128)(2,1)} %copy-done.10), custom_call_target="tpu_custom_call" | custom-call | flops 1000000000 | bytes 4194304 | tf_op jit(solution)/shard_map/pick/pallas_call | solution.py:171
  68.5 12.2 %all-to-all-start = ((bf16[64,24,384]{2,1,0:T(8,128)(2,1)}), bf16[64,24,384]{2,1,0:T(8,128)(2,1)S(1)}, u32[]{:S(2)}, u32[]{:S(2)}) async-start(bf16[64,24,384]{2,1,0:T(8,128)(2,1)} %bitcast.42), calls=%async_computation | async-start | bytes 2359296 | tf_op jit(solution)/shard_map/all_to_all | solution.py:301
  80.9 1.7 collective-permute-done.8
  85.3 2.2 %gather_fusion.1 = bf16[4,192,1280]{2,1,0:T(8,128)(2,1)S(1)} fusion(bf16[4,192,1280]{2,1,0:T(8,128)(2,1)} %pad_maximum_fusion, s32[1024]{0:T(1024)S(1)} %pad_clamp_fusion), kind=kCustom, calls=%fused_computation.1 | custom fusion | bytes 3932176 | tf_op jit(solution)/shard_map/jit(_take)/gather | solution.py:260
  87.5 2.3 %copy.20 = bf16[768,1280]{0,1:T(8,128)(2,1)} copy(bf16[768,1280]{1,0:T(8,128)(2,1)S(1)} %bitcast.36) | data formatting | bytes 3932160 | tf_op jit(solution)/shard_map/jit(_take)/gather | solution.py:260
  89.8 3.0 %select_bitcast_fusion = bf16[1280,768]{1,0:T(8,128)(2,1)} fusion(bf16[768,1280]{0,1:T(8,128)(2,1)} %copy.20, pred[768]{0:T(1024)(128)(4,1)S(1)} %broadcast_in_dim.54), kind=kLoop, calls=%fused_computation.4 | loop fusion | flops 983040 | bytes 3932928 | tf_op jit(solution)/shard_map/transpose | solution.py:306
  92.9 4.0 %reshape.126 = bf16[8,4,2,20,768]{4,3,2,1,0:T(8,128)(2,1)} reshape(bf16[1280,768]{1,0:T(8,128)(2,1)} %select_bitcast_fusion) | data formatting | bytes 3932160 | tf_op jit(solution)/shard_map/reshape | solution.py:306
  96.8 1.9 %copy.23 = bf16[2,8,4,20,768]{4,3,2,1,0:T(8,128)(2,1)S(1)} copy(bf16[2,8,4,20,768]{4,3,0,2,1:T(8,128)(2,1)} %bitcast.37) | data formatting | bytes 3932160
  98.8 1.7 pad.9.clone
  102.0 14.9 %all-gather.2.cloned.1.call-done = bf16[1536,384]{1,0:T(8,128)(2,1)} async-done(((bf16[192,384]{1,0:T(8,128)(2,1)}), bf16[1536,384]{1,0:T(8,128)(2,1)}) %all-gather.2.cloned.1.call-update) | async-done | bytes 1179664 | tf_op jit(solution)/shard_map/all_gather | solution.py:285
  116.9 2.1 %reshape.125.w_ref = bf16[1280,384]{1,0:T(8,128)(2,1)} reshape(bf16[64,20,384]{2,1,0:T(8,128)(2,1)} %bitcast.40) | data formatting | bytes 1966080 | tf_op jit(solution)/shard_map/reshape | solution.py:286
  119.1 3.4 %fusion.6.pred_ref = f32[768,384]{1,0:T(8,128)} fusion(bf16[768,1280]{1,0:T(8,128)(2,1)S(1)} %bitcast.39, bf16[1280,384]{1,0:T(8,128)(2,1)} %reshape.125.w_ref), kind=kOutput, calls=%fused_computation.43 | convolution fusion | flops 754974720 | bytes 4128768 | tf_op jit(solution)/shard_map/dot_general | solution.py:305
  123.5 6.1 %land.1 = (bf16[768,384]{1,0:T(8,128)(2,1)}, bf16[768,384]{1,0:T(8,128)(2,1)}, f32[768,384]{1,0:T(8,128)}) custom-call(s32[1]{0:T(128)} %bitcast.1.core_ref, s32[1,1536]{1,0:T(1,128)} %constant.71.clone.base_ref, bf16[1536,384]{1,0:T(8,128)(2,1)} %bitcast.41, f32[768,384]{1,0:T(8,128)} %fusion.6.pred_ref, bf16[2,768,768]{2,1,0:T(8,128)(2,1)} %bitcast.38), custom_call_target="tpu_custom_call" | custom-call | flops 2000000000 | bytes 8388608 | tf_op jit(solution)/shard_map/land/pallas_call | solution.py:201
  129.6 4.0 %grad.1 = (f32[192,1280]{1,0:T(8,128)}, bf16[192,1280]{1,0:T(8,128)(2,1)}, bf16[96,1280]{1,0:T(8,128)(2,1)}, bf16[96,1280]{1,0:T(8,128)(2,1)}, bf16[192,1280]{1,0:T(8,128)(2,1)}) custom-call(s32[1]{0:T(128)} %bitcast.x_ref, bf16[768,384]{1,0:T(8,128)(2,1)} %get-tuple-element.20.err_ref, bf16[1280,384]{1,0:T(8,128)(2,1)} %reshape.125.w_ref), custom_call_target="tpu_custom_call" | custom-call | flops 1000000000 | bytes 4194304 | tf_op jit(solution)/shard_map/grad/pallas_call | solution.py:236
  136.6 4.1 %collective-permute-start.12 = (bf16[96,1280]{1,0:T(8,128)(2,1)}, bf16[96,1280]{1,0:T(8,128)(2,1)S(1)}, u32[]{:S(2)}, u32[]{:S(2)}) collective-permute-start(bf16[96,1280]{1,0:T(8,128)(2,1)} %get-tuple-element.25), channel_id=1, source_target_pairs={{0,3},{1,0},{2,1},{3,2},{4,7},{5,4},{6,5},{7,6},{8,11},{9,8},{10,9... | collective-permute-start | bytes 737288 | tf_op jit(solution)/shard_map/ppermute | solution.py:249
  141.7 6.4 %all-to-all-start.2 = ((bf16[32,24,384]{2,1,0:T(8,128)(2,1)}), bf16[32,24,384]{2,1,0:T(8,128)(2,1)S(1)}, u32[]{:S(2)}, u32[]{:S(2)}) async-start(bf16[32,24,384]{2,1,0:T(8,128)(2,1)} %bitcast.22), calls=%async_computation.2 | async-start | bytes 1179648 | tf_op jit(solution)/shard_map/all_to_all | solution.py:314
  148.2 2.6 %collective-permute-start.13 = (bf16[192,1280]{1,0:T(8,128)(2,1)S(1)}, bf16[192,1280]{1,0:T(8,128)(2,1)S(1)}, u32[]{:S(2)}, u32[]{:S(2)}) collective-permute-start(bf16[192,1280]{1,0:T(8,128)(2,1)S(1)} %pad_maximum_fusion.4), channel_id=1, source_target_pairs={{0,3},{1,0},{2,1},{3,2},{4,7},{5,4},{6,5},{7,6},{8,11},{9,8},{10,9... | collective-permute-start | bytes 1474568 | tf_op jit(solution)/shard_map/ppermute | solution.py:252
  152.7 14.5 %all-to-all-done.2 = bf16[32,24,384]{2,1,0:T(8,128)(2,1)S(1)} async-done(((bf16[32,24,384]{2,1,0:T(8,128)(2,1)}), bf16[32,24,384]{2,1,0:T(8,128)(2,1)S(1)}, u32[]{:S(2)}, u32[]{:S(2)}) %all-to-all-start.2) | async-done | bytes 589856 | tf_op jit(solution)/shard_map/all_to_all | solution.py:314
  167.3 1.7 collective-permute-start.16
  169.0 2.4 %collective-permute-start.15 = (f32[20,320]{1,0:T(8,128)S(1)}, f32[20,320]{1,0:T(8,128)S(1)}, u32[]{:S(2)}, u32[]{:S(2)}) collective-permute-start(f32[20,320]{1,0:T(8,128)S(1)} %get-tuple-element.31), channel_id=1, source_target_pairs={{0,1},{1,2},{2,3},{3,0},{4,5},{5,6},{6,7},{7,4},{8,9},{9,10},{10,1... | collective-permute-start | bytes 76808 | tf_op jit(solution)/shard_map/ppermute | solution.py:257
  173.0 2.3 %collective-permute-done.17 = f32[20,320]{1,0:T(8,128)S(1)} collective-permute-done((f32[20,320]{1,0:T(8,128)S(1)}, f32[20,320]{1,0:T(8,128)S(1)}, u32[]{:S(2)}, u32[]{:S(2)}) %collective-permute-start.17) | collective-permute-done | bytes 25632 | tf_op jit(solution)/shard_map/ppermute | solution.py:257
  (88 shorter events, 25.5 us)
Async XLA Ops:
  7.2 6.5 %copy-start = (bf16[20,1280]{1,0:T(8,128)(2,1)S(1)}, bf16[20,1280]{1,0:T(8,128)(2,1)}, u32[]{:S(2)}) copy-start(bf16[20,1280]{1,0:T(8,128)(2,1)} %param.24) | copy-start | bytes 153604
  9.5 43.0 %collective-permute-start.1 = (s32[2,192]{1,0:T(2,128)S(1)}, s32[2,192]{1,0:T(2,128)S(1)}, u32[]{:S(2)}, u32[]{:S(2)}) collective-permute-start(s32[2,192]{1,0:T(2,128)S(1)} %get-tuple-element.33), channel_id=1, source_target_pairs={{0,2},{1,3},{2,0},{3,1},{4,6},{5,7},{6,4},{7,5},{8,10},{9,11},{10,... | collective-permute-start | bytes 4616 | tf_op jit(solution)/shard_map/ppermute | solution.py:257
  11.6 44.4 %collective-permute-start = (s32[2,192]{1,0:T(2,128)S(1)}, s32[2,192]{1,0:T(2,128)S(1)}, u32[]{:S(2)}, u32[]{:S(2)}) collective-permute-start(s32[2,192]{1,0:T(2,128)S(1)} %get-tuple-element.33), channel_id=1, source_target_pairs={{0,1},{1,2},{2,3},{3,0},{4,5},{5,6},{6,7},{7,4},{8,9},{9,10},{10,1... | collective-permute-start | bytes 4616 | tf_op jit(solution)/shard_map/ppermute | solution.py:257
  13.2 44.9 %collective-permute-start.2 = (s32[2,192]{1,0:T(2,128)S(1)}, s32[2,192]{1,0:T(2,128)S(1)}, u32[]{:S(2)}, u32[]{:S(2)}) collective-permute-start(s32[2,192]{1,0:T(2,128)S(1)} %get-tuple-element.33), channel_id=1, source_target_pairs={{0,3},{1,0},{2,1},{3,2},{4,7},{5,4},{6,5},{7,6},{8,11},{9,8},{10,9... | collective-permute-start | bytes 4616 | tf_op jit(solution)/shard_map/ppermute | solution.py:257
  14.4 48.3 %all-to-all-start.1 = ((bf16[8,24,384]{2,1,0:T(8,128)(2,1)}), bf16[8,24,384]{2,1,0:T(8,128)(2,1)S(1)}, u32[]{:S(2)}, u32[]{:S(2)}) async-start(bf16[8,24,384]{2,1,0:T(8,128)(2,1)} %broadcast_in_dim.52), calls=%async_computation.1 | async-start | bytes 294912 | tf_op jit(solution)/shard_map/all_to_all | solution.py:282
  18.9 98.0 %all-gather.2.cloned.1.call-start = ((), (), s32[]{:S(2)}) async-start(), calls=%async_computation.3 | async-start | bytes 1327104 | tf_op jit(solution)/shard_map/all_gather | solution.py:285
  35.5 12.9 %copy-start.8 = (bf16[384,640]{1,0:T(8,128)(2,1)S(1)}, bf16[384,640]{1,0:T(8,128)(2,1)}, u32[]{:S(2)}) copy-start(bf16[384,640]{1,0:T(8,128)(2,1)} %get-tuple-element.16) | copy-start | bytes 1474564
  35.5 12.9 %collective-permute-start.3 = (bf16[192,640]{1,0:T(8,128)(2,1)}, bf16[192,640]{1,0:T(8,128)(2,1)S(1)}, u32[]{:S(2)}, u32[]{:S(2)}) collective-permute-start(bf16[192,640]{1,0:T(8,128)(2,1)} %get-tuple-element.17), channel_id=1, source_target_pairs={{0,1},{1,2},{2,3},{3,0},{4,5},{5,6},{6,7},{7,4},{8,9},{9,10},{10,1... | collective-permute-start | bytes 737288 | tf_op jit(solution)/shard_map/ppermute | solution.py:248
  36.0 8.3 %collective-permute-start.5 = (bf16[192,640]{1,0:T(8,128)(2,1)}, bf16[192,640]{1,0:T(8,128)(2,1)S(1)}, u32[]{:S(2)}, u32[]{:S(2)}) collective-permute-start(bf16[192,640]{1,0:T(8,128)(2,1)} %get-tuple-element.19), channel_id=1, source_target_pairs={{0,3},{1,0},{2,1},{3,2},{4,7},{5,4},{6,5},{7,6},{8,11},{9,8},{10,9... | collective-permute-start | bytes 737288 | tf_op jit(solution)/shard_map/ppermute | solution.py:249
  45.4 18.0 %collective-permute-start.6 = (bf16[384,640]{1,0:T(8,128)(2,1)S(1)}, bf16[384,640]{1,0:T(8,128)(2,1)S(1)}, u32[]{:S(2)}, u32[]{:S(2)}) collective-permute-start(bf16[384,640]{1,0:T(8,128)(2,1)S(1)} %pad_maximum_fusion.2), channel_id=1, source_target_pairs={{0,3},{1,0},{2,1},{3,2},{4,7},{5,4},{6,5},{7,6},{8,11},{9,8},{10,9... | collective-permute-start | bytes 1474568 | tf_op jit(solution)/shard_map/ppermute | solution.py:252
  48.5 15.9 %collective-permute-start.4 = (bf16[384,640]{1,0:T(8,128)(2,1)S(1)}, bf16[384,640]{1,0:T(8,128)(2,1)}, u32[]{:S(2)}, u32[]{:S(2)}) collective-permute-start(bf16[384,640]{1,0:T(8,128)(2,1)S(1)} %pad_maximum_fusion.1), channel_id=1, source_target_pairs={{0,1},{1,2},{2,3},{3,0},{4,5},{5,6},{6,7},{7,4},{8,9},{9,10},{10,1... | collective-permute-start | bytes 1474568 | tf_op jit(solution)/shard_map/ppermute | solution.py:252
  52.5 28.4 %collective-permute-start.9 = (bf16[192,1280]{1,0:T(8,128)(2,1)}, bf16[192,1280]{1,0:T(8,128)(2,1)S(1)}, u32[]{:S(2)}, u32[]{:S(2)}) collective-permute-start(bf16[192,1280]{1,0:T(8,128)(2,1)} %student.1), channel_id=1, source_target_pairs={{0,3},{1,0},{2,1},{3,2},{4,7},{5,4},{6,5},{7,6},{8,11},{9,8},{10,9... | collective-permute-start | bytes 1474568 | tf_op jit(solution)/shard_map/ppermute | solution.py:257
  56.0 26.6 %collective-permute-start.8 = (bf16[192,1280]{1,0:T(8,128)(2,1)}, bf16[192,1280]{1,0:T(8,128)(2,1)S(1)}, u32[]{:S(2)}, u32[]{:S(2)}) collective-permute-start(bf16[192,1280]{1,0:T(8,128)(2,1)} %student.1), channel_id=1, source_target_pairs={{0,2},{1,3},{2,0},{3,1},{4,6},{5,7},{6,4},{7,5},{8,10},{9,11},{10,... | collective-permute-start | bytes 1474568 | tf_op jit(solution)/shard_map/ppermute | solution.py:257
  58.2 25.5 %collective-permute-start.7 = (bf16[192,1280]{1,0:T(8,128)(2,1)}, bf16[192,1280]{1,0:T(8,128)(2,1)S(1)}, u32[]{:S(2)}, u32[]{:S(2)}) collective-permute-start(bf16[192,1280]{1,0:T(8,128)(2,1)} %student.1), channel_id=1, source_target_pairs={{0,1},{1,2},{2,3},{3,0},{4,5},{5,6},{6,7},{7,4},{8,9},{9,10},{10,1... | collective-permute-start | bytes 1474568 | tf_op jit(solution)/shard_map/ppermute | solution.py:257
  63.4 1.0 copy-start.10
  68.5 15.2 %copy-start.6 = (bf16[192,1280]{1,0:T(8,128)(2,1)S(1)}, bf16[192,1280]{1,0:T(8,128)(2,1)}, u32[]{:S(2)}) copy-start(bf16[192,1280]{1,0:T(8,128)(2,1)} %student.1) | copy-start | bytes 1474564
  68.5 54.0 %all-to-all-start = ((bf16[64,24,384]{2,1,0:T(8,128)(2,1)}), bf16[64,24,384]{2,1,0:T(8,128)(2,1)S(1)}, u32[]{:S(2)}, u32[]{:S(2)}) async-start(bf16[64,24,384]{2,1,0:T(8,128)(2,1)} %bitcast.42), calls=%async_computation | async-start | bytes 2359296 | tf_op jit(solution)/shard_map/all_to_all | solution.py:301
  102.0 17.0 %copy-start.1 = (bf16[4,192,1280]{2,1,0:T(8,128)(2,1)S(1)}, bf16[4,192,1280]{2,1,0:T(8,128)(2,1)}, u32[]{:S(2)}) copy-start(bf16[4,192,1280]{2,1,0:T(8,128)(2,1)} %broadcast_select_fusion) | copy-start | bytes 5898244
  122.5 1.0 copy-start.2
  129.6 11.1 %collective-permute-start.14 = (bf16[768,384]{1,0:T(8,128)(2,1)}, bf16[768,384]{1,0:T(8,128)(2,1)S(1)}, u32[]{:S(2)}, u32[]{:S(2)}) collective-permute-start(bf16[768,384]{1,0:T(8,128)(2,1)} %get-tuple-element.27), channel_id=1, source_target_pairs={{0,4},{4,0},{1,5},{5,1},{2,6},{6,2},{3,7},{7,3},{8,12},{12,8},{9,1... | collective-permute-start | bytes 1769480 | tf_op jit(solution)/shard_map/ppermute | solution.py:313
  129.6 11.1 %copy-start.3 = (f32[768,384]{1,0:T(8,128)S(1)}, f32[768,384]{1,0:T(8,128)}, u32[]{:S(2)}) copy-start(f32[768,384]{1,0:T(8,128)} %get-tuple-element.26) | copy-start | bytes 3538948
  134.6 13.5 %copy-start.9 = (bf16[192,1280]{1,0:T(8,128)(2,1)S(1)}, bf16[192,1280]{1,0:T(8,128)(2,1)}, u32[]{:S(2)}) copy-start(bf16[192,1280]{1,0:T(8,128)(2,1)} %get-tuple-element.24) | copy-start | bytes 1474564
  135.6 15.2 %collective-permute-start.10 = (bf16[96,1280]{1,0:T(8,128)(2,1)}, bf16[96,1280]{1,0:T(8,128)(2,1)}, u32[]{:S(2)}, u32[]{:S(2)}) collective-permute-start(bf16[96,1280]{1,0:T(8,128)(2,1)} %get-tuple-element.23), channel_id=1, source_target_pairs={{0,1},{1,2},{2,3},{3,0},{4,5},{5,6},{6,7},{7,4},{8,9},{9,10},{10,1... | collective-permute-start | bytes 737288 | tf_op jit(solution)/shard_map/ppermute | solution.py:248
  136.6 11.5 %collective-permute-start.12 = (bf16[96,1280]{1,0:T(8,128)(2,1)}, bf16[96,1280]{1,0:T(8,128)(2,1)S(1)}, u32[]{:S(2)}, u32[]{:S(2)}) collective-permute-start(bf16[96,1280]{1,0:T(8,128)(2,1)} %get-tuple-element.25), channel_id=1, source_target_pairs={{0,3},{1,0},{2,1},{3,2},{4,7},{5,4},{6,5},{7,6},{8,11},{9,8},{10,9... | collective-permute-start | bytes 737288 | tf_op jit(solution)/shard_map/ppermute | solution.py:249
  141.7 9.2 %copy-start.7 = (bf16[192,1280]{1,0:T(8,128)(2,1)S(1)}, bf16[192,1280]{1,0:T(8,128)(2,1)}, u32[]{:S(2)}) copy-start(bf16[192,1280]{1,0:T(8,128)(2,1)} %get-tuple-element.22) | copy-start | bytes 1474564
  141.7 25.5 %all-to-all-start.2 = ((bf16[32,24,384]{2,1,0:T(8,128)(2,1)}), bf16[32,24,384]{2,1,0:T(8,128)(2,1)S(1)}, u32[]{:S(2)}, u32[]{:S(2)}) async-start(bf16[32,24,384]{2,1,0:T(8,128)(2,1)} %bitcast.22), calls=%async_computation.2 | async-start | bytes 1179648 | tf_op jit(solution)/shard_map/all_to_all | solution.py:314
  148.0 23.4 %copy-start.4 = (f32[192,1280]{1,0:T(8,128)S(1)}, f32[192,1280]{1,0:T(8,128)}, u32[]{:S(2)}) copy-start(f32[192,1280]{1,0:T(8,128)} %get-tuple-element.21) | copy-start | bytes 2949124
  148.2 23.2 %collective-permute-start.13 = (bf16[192,1280]{1,0:T(8,128)(2,1)S(1)}, bf16[192,1280]{1,0:T(8,128)(2,1)S(1)}, u32[]{:S(2)}, u32[]{:S(2)}) collective-permute-start(bf16[192,1280]{1,0:T(8,128)(2,1)S(1)} %pad_maximum_fusion.4), channel_id=1, source_target_pairs={{0,3},{1,0},{2,1},{3,2},{4,7},{5,4},{6,5},{7,6},{8,11},{9,8},{10,9... | collective-permute-start | bytes 1474568 | tf_op jit(solution)/shard_map/ppermute | solution.py:252
  152.7 18.7 %collective-permute-start.11 = (bf16[192,1280]{1,0:T(8,128)(2,1)}, bf16[192,1280]{1,0:T(8,128)(2,1)S(1)}, u32[]{:S(2)}, u32[]{:S(2)}) collective-permute-start(bf16[192,1280]{1,0:T(8,128)(2,1)} %pad_maximum_fusion.3), channel_id=1, source_target_pairs={{0,1},{1,2},{2,3},{3,0},{4,5},{5,6},{6,7},{7,4},{8,9},{9,10},{10,1... | collective-permute-start | bytes 1474568 | tf_op jit(solution)/shard_map/ppermute | solution.py:252
  167.3 5.5 %collective-permute-start.16 = (f32[20,320]{1,0:T(8,128)S(1)}, f32[20,320]{1,0:T(8,128)S(1)}, u32[]{:S(2)}, u32[]{:S(2)}) collective-permute-start(f32[20,320]{1,0:T(8,128)S(1)} %get-tuple-element.31), channel_id=1, source_target_pairs={{0,2},{1,3},{2,0},{3,1},{4,6},{5,7},{6,4},{7,5},{8,10},{9,11},{10,... | collective-permute-start | bytes 76808 | tf_op jit(solution)/shard_map/ppermute | solution.py:257
  169.0 4.0 %collective-permute-start.15 = (f32[20,320]{1,0:T(8,128)S(1)}, f32[20,320]{1,0:T(8,128)S(1)}, u32[]{:S(2)}, u32[]{:S(2)}) collective-permute-start(f32[20,320]{1,0:T(8,128)S(1)} %get-tuple-element.31), channel_id=1, source_target_pairs={{0,1},{1,2},{2,3},{3,0},{4,5},{5,6},{6,7},{7,4},{8,9},{9,10},{10,1... | collective-permute-start | bytes 76808 | tf_op jit(solution)/shard_map/ppermute | solution.py:257
  171.4 4.0 %collective-permute-start.17 = (f32[20,320]{1,0:T(8,128)S(1)}, f32[20,320]{1,0:T(8,128)S(1)}, u32[]{:S(2)}, u32[]{:S(2)}) collective-permute-start(f32[20,320]{1,0:T(8,128)S(1)} %get-tuple-element.31), channel_id=1, source_target_pairs={{0,3},{1,0},{2,1},{3,2},{4,7},{5,4},{6,5},{7,6},{8,11},{9,8},{10,9... | collective-permute-start | bytes 76808 | tf_op jit(solution)/shard_map/ppermute | solution.py:257
  (1 other events, 0.7 us)
Sparse Core Ops, SparseCore 0:
  63.5 53.3 all-gather.1

commit v2 on v1

v2 whole, which is shorter than its diff:
```python
import functools
import math

import jax
import jax.numpy as jnp
import numpy as np
from jax import lax
from jax.experimental import pallas as pl
from jax.experimental.pallas import tpu as pltpu
from jax.sharding import Mesh, PartitionSpec as P

HDT = 128
HDS = 64
LOG2E = 1.4426950408889634
BIG = 1e30
BF = jnp.bfloat16
F32 = jnp.float32
DP = ("z", "y", "core")
NT = (((1,), (1,)), ((), ()))
TN = (((0,), (0,)), ((), ()))
WIDE = 384
TABLE = 16
MIB = 1024 * 1024


def ring(n, k):
    return [(i, (i + k) % n) for i in range(n)]


def params(mib):
    return pltpu.CompilerParams(vmem_limit_bytes=mib * MIB)


def segment_columns(ids):
    n = ids.shape[1]
    lane = lax.broadcasted_iota(jnp.int32, (128, n), 0)
    hot = jnp.transpose((lane == ids).astype(F32))
    return hot.astype(BF), ((hot - 1.0) * BIG).astype(BF)


def softmax_rows(scores, scale):
    top = jnp.max(scores, axis=1, keepdims=True)
    return jnp.exp2((scores - top) * scale).astype(BF)


def send_table(owner, slot, wide):
    n = owner.shape[1]
    across = owner.astype(F32)
    down = jnp.transpose(jnp.broadcast_to(across, (128, n)))[:, 0:1]
    before = lax.broadcasted_iota(jnp.int32, (n, n), 0) < lax.broadcasted_iota(jnp.int32, (n, n), 1)
    place = jnp.sum(jnp.where(jnp.logical_and(down == across, before), 1.0, 0.0), axis=0, keepdims=True)
    row = lax.broadcasted_iota(jnp.int32, (TABLE, n), 0)
    table = jnp.where(row == 0, across, jnp.where(row == 1, place, jnp.where(row == 2, slot.astype(F32), 0.0)))
    return jnp.concatenate([table, jnp.zeros((TABLE, wide - n), F32)], axis=1).astype(BF)


def teacher_kernel(x_ref, ids_ref, sends_ref, w_ref, q_ref, k_ref, v_ref, map_hbm, out_ref, mine_ref, qx, kx, ve, ctx,
                   map_ref, sem):
    step = pl.program_id(0)
    fetch = pltpu.make_async_copy(map_hbm, map_ref, sem)
    rows = ctx.shape[0]
    half = rows // 2
    scale = LOG2E / math.sqrt(HDT)

    @pl.when(step == 0)
    def _():
        fetch.start()
        hot, far = segment_columns(ids_ref[...])
        qx[...] = hot
        kx[...] = far
        ve[:, HDT:] = jnp.ones((rows, HDT), BF)
        table = send_table(sends_ref[0:1, :], sends_ref[1:2, :], out_ref.shape[2])
        for n in range(4):
            out_ref[n, half:, :] = table
        weight = w_ref[...].astype(F32)
        block = weight.shape[1] // 4
        rest = jnp.zeros((weight.shape[0], WIDE - block), F32)
        below = jnp.zeros((mine_ref.shape[0] - weight.shape[0], WIDE), F32)
        for n in range(4):
            @pl.when(x_ref[0] == n)
            def _():
                part = jnp.concatenate([weight[:, n * block:(n + 1) * block], rest], axis=1)
                mine_ref[...] = jnp.concatenate([part, below], axis=0).astype(BF)

    for h in range(2):
        cols = slice(h * HDT, (h + 1) * HDT)
        ke = jnp.concatenate([k_ref[:, cols], kx[...]], axis=1)
        ve[:, :HDT] = v_ref[:, cols]
        for r in range(0, rows, 256):
            qe = jnp.concatenate([q_ref[r:r + 256, cols], qx[r:r + 256, :]], axis=1)
            s = lax.dot_general(qe, ke, NT, preferred_element_type=F32)
            p = softmax_rows(s, scale)
            o = jnp.dot(p, ve[...], preferred_element_type=F32)
            c = (o[:, :HDT] / o[:, HDT:]).astype(BF)
            ctx[r:r + 256, pl.ds(pl.multiple_of(step * 256 + h * HDT, HDT), HDT)] = c

    @pl.when(step == pl.num_programs(0) - 1)
    def _():
        fetch.wait()
        block = map_ref.shape[1] // 4
        for r in range(0, half, 192):
            a = jnp.dot(ctx[r:r + 192, :], map_ref[...], preferred_element_type=F32)
            b = jnp.dot(ctx[half + r:half + r + 192, :], map_ref[...], preferred_element_type=F32)
            for n in range(4):
                out_ref[n, r:r + 192, :] = jnp.concatenate(
                    [a[:, n * block:(n + 1) * block], b[:, n * block:(n + 1) * block]], axis=1
                ).astype(BF)


def teacher(x, ids, sends, weight, q, k, v, tmap):
    rows, width = q.shape
    out = tmap.shape[1]
    half = rows // 2
    wide = out // 2
    pair = 2 * HDT
    steps = width // pair
    shapes = [(4, half + TABLE, wide), (weight.shape[0] + -weight.shape[0] % 8, WIDE)]
    return pl.pallas_call(
        teacher_kernel,
        grid=(steps,),
        in_specs=[
            pl.BlockSpec(memory_space=pltpu.SMEM),
            pl.BlockSpec((1, rows), lambda i: (0, 0)),
            pl.BlockSpec(sends.shape, lambda i: (0, 0)),
            pl.BlockSpec(weight.shape, lambda i: (0, 0)),
            pl.BlockSpec((rows, pair), lambda i: (0, i)),
            pl.BlockSpec((rows, pair), lambda i: (0, i)),
            pl.BlockSpec((rows, pair), lambda i: (0, i)),
            pl.BlockSpec(memory_space=pl.ANY),
        ],
        out_specs=[pl.BlockSpec(shapes[0], lambda i: (0, 0, 0)), pl.BlockSpec(shapes[1], lambda i: (0, 0))],
        out_shape=[jax.ShapeDtypeStruct(shape, BF) for shape in shapes],
        scratch_shapes=[
            pltpu.VMEM((rows, 128), BF),
            pltpu.VMEM((rows, 128), BF),
            pltpu.VMEM((rows, pair), BF),
            pltpu.VMEM((rows, width), BF),
            pltpu.VMEM((width, out), BF),
            pltpu.SemaphoreType.DMA,
        ],
        compiler_params=params(60),
        cost_estimate=pl.CostEstimate(flops=10 * 10**9, bytes_accessed=10 * 2**20, transcendentals=6 * 10**6),
        name="teacher",
    )(x, ids, sends, weight, q, k, v, tmap)


def student_kernel(ids_ref, q_ref, k_ref, v_ref, o_ref):
    rows, width = q_ref.shape
    scale = LOG2E / math.sqrt(HDS)
    hot, far = segment_columns(ids_ref[...])
    low = lax.broadcasted_iota(jnp.int32, (rows, 128), 1) < HDS
    ones = jnp.ones((rows, 128), BF)
    for g in range(0, width, 128):
        cols = slice(g, g + 128)
        ke = jnp.concatenate([k_ref[:, cols], far], axis=1)
        ve = jnp.concatenate([v_ref[:, cols], ones], axis=1)
        q = q_ref[:, cols]
        done = []
        for keep in (low, jnp.logical_not(low)):
            qe = jnp.concatenate([jnp.where(keep, q, jnp.zeros_like(q)), hot], axis=1)
            s = lax.dot_general(qe, ke, NT, preferred_element_type=F32)
            o = jnp.dot(softmax_rows(s, scale), ve, preferred_element_type=F32)
            done.append(o[:, :128] / o[:, 128:])
        o_ref[:, cols] = jnp.where(low, done[0], done[1]).astype(BF)


def student(ids, q, k, v):
    return pl.pallas_call(
        student_kernel,
        out_shape=jax.ShapeDtypeStruct(q.shape, BF),
        compiler_params=params(24),
        cost_estimate=pl.CostEstimate(flops=10**9, bytes_accessed=2 * 2**20, transcendentals=10**6),
        name="student",
    )(ids, q, k, v)


def select_kernel(capacity, unit, parts_ref, o_ref, rows_ref):
    half = parts_ref.shape[1] - TABLE
    block = parts_ref.shape[2] // 2
    quarter = half // 2
    table = [parts_ref[n, half:, :quarter].astype(F32) for n in range(4)]
    idx = jnp.concatenate(
        [t[0:1, :] * unit + t[1:2, :] + n * capacity for n, t in enumerate(table)], axis=1
    ).astype(jnp.int32)
    slot = jnp.concatenate([t[2:3, :] for t in table], axis=1)
    mark = jnp.transpose(jnp.broadcast_to(slot + 1.0, (128, 2 * half)))[:, :WIDE - block]
    for r in (0, quarter):
        a, b, c, d = (parts_ref[n, r:r + quarter, :].astype(F32) for n in range(4))
        total = (a + b) + (c + d)
        for c, m in ((0, r), (block, half + r)):
            rows_ref[m:m + quarter, :] = jnp.concatenate(
                [total[:, c:c + block], mark[m:m + quarter, :]], axis=1
            ).astype(BF)
    for r in range(0, o_ref.shape[0], 256):
        row = lax.broadcasted_iota(jnp.int32, (256, 2 * half), 0) + r
        hot = (row == idx).astype(F32).astype(BF)
        o_ref[r:r + 256, :] = jnp.dot(hot, rows_ref[...], preferred_element_type=F32).astype(BF)


def select(parts, owners, capacity):
    unit = 4 * capacity
    return pl.pallas_call(
        functools.partial(select_kernel, capacity, unit),
        out_shape=jax.ShapeDtypeStruct((owners * unit, WIDE), BF),
        scratch_shapes=[pltpu.VMEM((2 * (parts.shape[1] - TABLE), WIDE), BF)],
        compiler_params=params(16),
        cost_estimate=pl.CostEstimate(flops=10**9, bytes_accessed=4 * 2**20, transcendentals=0),
        name="pick",
    )(parts)


def project_kernel(unit, padded, at_ref, c0_ref, c1_ref, c2_ref, c3_ref, c4_ref, near_ref, other_ref, pred_ref, ctxt_ref, w_ref, ctx,
                   raw, rows):
    count = near_ref.shape[0] // padded
    raw[:count] = near_ref[...].astype(F32).reshape(count, padded, WIDE)
    raw[count:] = other_ref[...].astype(F32).reshape(count, padded, WIDE)
    z, y, c = at_ref[0], at_ref[1], at_ref[2]
    row = 0
    for m in range(8):
        d = lax.rem(z - m + 8, 8)
        turn = (d % 2) * 4 + d // 2
        for n in range(4):
            for o in range(2):
                at = lax.rem(c + o, 2) * count + lax.rem(y - n + 4, 4) * 8 + turn
                rows[row:row + unit, :] = raw[at, :unit, :]
                row += unit
    w_ref[...] = rows[...].astype(BF)
    start = 0
    for c_ref in (c0_ref, c1_ref, c2_ref, c3_ref, c4_ref):
        ctx[start:start + c_ref.shape[0], :] = c_ref[...]
        start += c_ref.shape[0]
    for c in range(0, ctx.shape[1], 256):
        for r in range(0, ctx.shape[0], 256):
            ctxt_ref[c:c + 256, r:r + 256] = jnp.transpose(ctx[r:r + 256, c:c + 256].astype(F32)).astype(BF)
    pred_ref[...] = jnp.dot(ctx[...], w_ref[...], preferred_element_type=F32)


def project(at, pieces, near, other, unit, padded):
    quarter, width = pieces[0].shape
    vm = pl.BlockSpec(memory_space=pltpu.VMEM)
    return pl.pallas_call(
        functools.partial(project_kernel, unit, padded),
        in_specs=[pl.BlockSpec(memory_space=pltpu.SMEM)] + [vm] * 7,
        out_shape=[
            jax.ShapeDtypeStruct((4 * quarter, WIDE), F32),
            jax.ShapeDtypeStruct((width, 4 * quarter), BF),
            jax.ShapeDtypeStruct((width, WIDE), BF),
        ],
        scratch_shapes=[
            pltpu.VMEM((4 * quarter, width), BF),
            pltpu.VMEM((width // unit, padded, WIDE), F32),
            pltpu.VMEM((width, WIDE), F32),
        ],
        compiler_params=params(60),
        cost_estimate=pl.CostEstimate(flops=10**9, bytes_accessed=8 * 2**20, transcendentals=0),
        name="project",
    )(at, *pieces, near, other)


def land_kernel(unit, place_ref, t_ref, arrived_ref, pred_ref, ctxt_ref, err_ref, other_ref, own_ref, blocks):
    rows = err_ref.shape[0]
    quarter = rows // 4
    block = WIDE - 64
    slot = jnp.transpose(arrived_ref[:, 256:].astype(F32))[64:65, :].astype(jnp.int32)
    base = jnp.bitwise_and(place_ref[0] + 4 - t_ref[...], 3) * quarter - 1
    dst = jnp.where(slot > 0, slot + base, -1)
    valid = lax.broadcasted_iota(jnp.int32, (256, WIDE), 1) < block
    for r in range(0, rows, 256):
        row = lax.broadcasted_iota(jnp.int32, (256, dst.shape[1]), 0) + r
        hot = (row == dst).astype(F32).astype(BF)
        target = jnp.dot(hot, arrived_ref[...], preferred_element_type=F32)
        err_ref[r:r + 256, :] = jnp.where(valid, pred_ref[r:r + 256, :] - target, 0.0).astype(BF)
    n = ctxt_ref.shape[0] // (2 * unit)
    chunk = 4 * 2 * unit
    blocks[...] = jnp.zeros_like(blocks)
    for i in range(0, 2 * n, 8):
        term = jnp.dot(ctxt_ref[i * unit:i * unit + chunk, :], err_ref[...], preferred_element_type=F32)
        for j in range(8):
            blocks[j % 2, (i + j) // 2, :unit, :] = term[j * unit:(j + 1) * unit, :]
    core = place_ref[1]
    other_ref[...] = blocks[1 - core].reshape(other_ref.shape).astype(BF)
    own_ref[...] = blocks[core].reshape(own_ref.shape)


def land(place, kinds, arrived, pred, ctxt, unit, padded):
    rows = pred.shape[0]
    n = ctxt.shape[0] // (2 * unit)
    vm = pl.BlockSpec(memory_space=pltpu.VMEM)
    return pl.pallas_call(
        functools.partial(land_kernel, unit),
        in_specs=[pl.BlockSpec(memory_space=pltpu.SMEM), vm, vm, vm, vm],
        out_shape=[
            jax.ShapeDtypeStruct((rows, WIDE), BF),
            jax.ShapeDtypeStruct((n * padded, WIDE), BF),
            jax.ShapeDtypeStruct((n * padded, WIDE), F32),
        ],
        scratch_shapes=[pltpu.VMEM((2, n, padded, WIDE), F32)],
        compiler_params=params(24),
        cost_estimate=pl.CostEstimate(flops=2 * 10**9, bytes_accessed=8 * 2**20, transcendentals=0),
        name="land",
    )(place, kinds, arrived, pred, ctxt)


def grad_kernel(err_ref, w_ref, own_ref, left_ref, far_ref, right_ref):
    quarter = own_ref.shape[0]
    for k, ref in enumerate((own_ref, left_ref, far_ref, right_ref)):
        part = lax.dot_general(err_ref[k * quarter:(k + 1) * quarter, :], w_ref[...], NT, preferred_element_type=F32)
        ref[...] = part.astype(ref.dtype)


def grad_parts(err, weight):
    quarter = err.shape[0] // 4
    width = weight.shape[0]
    return pl.pallas_call(
        grad_kernel,
        out_shape=[jax.ShapeDtypeStruct((quarter, width), t) for t in (F32, BF, BF, BF)],
        compiler_params=params(16),
        cost_estimate=pl.CostEstimate(flops=10**9, bytes_accessed=4 * 2**20, transcendentals=0),
        name="grad",
    )(err, weight)


def after(value, *earlier):
    return lax.optimization_barrier((value,) + earlier)[0]


def go(a, k, axis="tensor"):
    return lax.ppermute(a, axis, ring(lax.axis_size(axis), k))


def add(a, b):
    return (a.astype(F32) + b.astype(F32)).astype(BF)


def pieces_x(a):
    return [a] + [go(a, k) for k in (1, 2, 3)]


def local(
    t_query, t_key, t_value, t_segments, teacher_map, send_owner, send_slot, s_query, s_key, s_value, s_segments, s_weight
):
    x = lax.axis_index("tensor")
    core = lax.axis_index("core")
    rows = send_owner.shape[0]
    width = s_weight.shape[1]
    n_z, n_y, n_c = (lax.axis_size(a) for a in DP)
    owners = n_z * n_y * n_c
    capacity = 2 * rows // owners
    block = width // 4
    unit = 4 * capacity
    place2 = jnp.stack([x, core]).astype(jnp.int32)
    xs = x.astype(jnp.int32).reshape(1)
    own_rows = s_weight.shape[0]
    padded = own_rows + -own_rows % 8

    sends = jnp.stack([send_owner, send_slot])
    parts, mine = teacher(xs, t_segments, sends, s_weight, t_query, t_key, t_value, teacher_map)
    parts = lax.all_to_all(parts, "tensor", 0, 0, tiled=True)
    outgoing = select(parts, owners, capacity)

    far = jnp.concatenate([mine] + [go(mine, k, "z") for k in (2, 4, 6)])
    far = jnp.concatenate([far, go(far, 1, "z")])
    first = go(far, 1, "y")
    last = go(far, 3, "y")
    context = student(s_segments, s_query, s_key, after(s_value, mine))

    outgoing, far, first, last, context = lax.optimization_barrier((outgoing, far, first, last, context))
    arrived = lax.all_to_all(outgoing, DP, 0, 0, tiled=True)

    right = go(context, 1)
    left = go(context, 3)
    contexts = (context, right, go(right[:rows // 2], 1), go(left[rows // 2:], 3), left)
    half = far.shape[0] // 2
    near = jnp.concatenate([far, first, go(first[:half], 1, "y"), go(last[half:], 3, "y"), last])
    where = jnp.stack([lax.axis_index(a) for a in DP]).astype(jnp.int32)
    prediction, turned, weight = project(where, contexts, near, go(near, 1, "core"), own_rows, padded)

    kinds = np.array([[(r % unit) // capacity for r in range(owners * unit)]], np.int32)
    err, other, term = land(place2, jnp.asarray(kinds), arrived, prediction, turned, own_rows, padded)
    own, *parts = grad_parts(err, weight)

    other, parts = lax.optimization_barrier((go(other, 1, "core"), parts))
    term = add(term, other)
    terms = lax.all_to_all(term, ("z", "y"), 0, 0, tiled=True)
    terms = terms.reshape(n_z * n_y, padded, WIDE)[:, :own_rows, :block]
    summed = jnp.sum(terms.astype(F32), axis=0) * (1.0 / math.sqrt(4 * rows * owners))
    whole = jnp.stack(pieces_x(summed))
    order = lax.rem(x - jnp.arange(4) + 4, 4)
    grad_weight = jnp.transpose(jnp.take(whole, order, axis=0), (1, 0, 2)).reshape(own_rows, width)

    grad_context = own + sum(go(part, 4 - k).astype(F32) for k, part in enumerate(parts, 1))
    return (grad_context, grad_weight)


def solution(mesh):
    fine = Mesh(mesh.devices.reshape(8, 4, 2, 4), DP + ("tensor",))
    both = DP + ("tensor",)
    placed = (
        P(DP, "tensor"),
        P(DP, "tensor"),
        P(DP, "tensor"),
        P(DP, None),
        P("tensor", None),
        P(both),
        P(both),
        P(both, None),
        P(both, None),
        P(both, None),
        P(both, None),
        P(DP, None),
    )
    return jax.shard_map(
        local, mesh=fine, in_specs=placed, out_specs=(P(both, None), P(DP, None)), check_vma=False
    )
```

time: 185 us -> 142 us (0.77)
  between operations: 14.3 us -> 0.89 us
  local copies, waits for them, and re-layouts: 24.1 us -> 12.7 us
  waiting for transfers between devices: 40.2 us -> 29.6 us
  other arithmetic: 13.9 us -> 5.46 us
  starting transfers between devices: 53.1 us -> 60.7 us
  Pallas kernels: 34.6 us -> 30.2 us
  matrix products: 3.42 us -> 0 us
    all_gather x1 -> x0, waiting for transfers between devices: 14.9 us -> none  [local(): weight = lax.all_gather(near, 'z', axis=0, tiled=True)]
    ppermute x18 -> x20, starting transfers between devices: 30.1 us -> 38.8 us  [go(): return lax.ppermute(a, axis, ring(lax.axis_size(axis), k))]
    reshape x3 -> x1, local copies, waits for them, and re-layouts: 6.86 us -> 0.77 us  [local(): jnp.transpose(jnp.take(whole, order, axis=0), (1, 0, 2))]
    gather x4 -> x1, local copies, waits for them, and re-layouts: 5.69 us -> 0.56 us  [local(): jnp.take(whole, order, axis=0)]
    all_to_all x1, waiting for transfers between devices: 0.01 us -> 4.85 us  [local(): arrived = lax.all_to_all(outgoing, DP, 0, 0, tiled=True)]
    unnamed x23 -> x36, local copies, waits for them, and re-layouts: 3.65 us -> 7.99 us
    dot_general x1 -> x0, matrix products: 3.42 us -> none  [local(): prediction = jnp.dot(contexts, weight, preferred_element_type=F32)]
    transpose x1 -> x0, other arithmetic: 3.03 us -> none  [local(): turned = contexts.T.reshape(n_z, n_y, n_c, own_rows, 4 * rows)]
  transfers between devices with their start and end apart: 22 -> 23, of which waited for: 9 -> 10; matrix products, arithmetic and copies ran while one was open for 20% -> 8% of each run, Pallas kernels for 16% -> 8%
where the time goes in v2:
time: 142 us; the launch traced here: 140 us
  starting transfers between devices  60.7 us (43%)
  Pallas kernels  30.2 us (21%)
  waiting for transfers between devices  29.6 us (21%)
  local copies, waits for them, and re-layouts  12.7 us (9%)
  other arithmetic  5.46 us (4%)
    ppermute x20, starting transfers between devices, go(): return lax.ppermute(a, axis, ring(lax.axis_size(axis), k))  38.8 us
    pallas_call x1, Pallas kernels, teacher(): pl.pallas_call(teacher_kernel, grid=(steps,), in_specs=[pl.BlockSpec(memo...  15.4 us
    ppermute x20, waiting for transfers between devices, go(): return lax.ppermute(a, axis, ring(lax.axis_size(axis), k))  13.2 us
    all_to_all x1, waiting for transfers between devices, local(): terms = lax.all_to_all(term, ('z', 'y'), 0, 0, tiled=True)  11.5 us
    all_to_all x1, starting transfers between devices, local(): arrived = lax.all_to_all(outgoing, DP, 0, 0, tiled=True)  11 us
    unnamed x36, local copies, waits for them, and re-layouts  7.99 us
    all_to_all x1, starting transfers between devices, local(): parts = lax.all_to_all(parts, 'tensor', 0, 0, tiled=True)  5.93 us
    pallas_call x1, Pallas kernels, project(): pl.pallas_call(functools.partial(project_kernel, unit, padded), in_specs=...  5.34 us
  transfers between devices with their start and end apart: 23, of which 10 were waited for; matrix products, arithmetic and copies ran while one was open for 8% of the time, Pallas kernels for 8%

profile of v2, /device:TPU:2, one launch (start us, length us, event | category | flops | bytes accessed | tf_op | source)
XLA Modules:
  0.0 139.6 jit_solution(18135711148164185117)
XLA Ops:
  1.9 15.4 %teacher.1 = (bf16[4,400,640]{2,1,0:T(8,128)(2,1)}, bf16[24,384]{1,0:T(8,128)(2,1)}) custom-call(s32[1]{0:T(128)} %bitcast.x_ref, s32[1,768]{1,0:T(1,128)} %ids_ref.2, s32[2,192]{1,0:T(2,128)} %pad_add_fusion.sends_ref, bf16[20,1280]{1,0:T(8,128)(2,1)} %w_ref.1, bf16[768,1280]{1,0:T(8,128)(2,1)} %q_ref.2, bf16[768,1280]{1,0:T(8,128)(2,1)} %k_ref.2, ...), custom_call_target="tpu_custom_call" | custom-call | flops 10000000000 | bytes 10485760 | tf_op jit(solution)/shard_map/teacher/pallas_call | solution.py:118
  17.4 5.9 %all-to-all-start = ((bf16[4,400,640]{2,1,0:T(8,128)(2,1)}), bf16[4,400,640]{2,1,0:T(8,128)(2,1)S(1)}, u32[]{:S(2)}, u32[]{:S(2)}) async-start(bf16[4,400,640]{2,1,0:T(8,128)(2,1)} %get-tuple-element.24), calls=%async_computation | async-start | bytes 4096000 | tf_op jit(solution)/shard_map/all_to_all | solution.py:358
  23.3 2.3 %collective-permute-start = (bf16[24,384]{1,0:T(8,128)(2,1)S(1)}, bf16[24,384]{1,0:T(8,128)(2,1)S(1)}, u32[]{:S(2)}, u32[]{:S(2)}) collective-permute-start(bf16[24,384]{1,0:T(8,128)(2,1)S(1)} %copy-done.12), channel_id=1, source_target_pairs={{0,64},{32,96},{64,128},{96,160},{128,192},{160,224},{192,0},{224,... | collective-permute-start | bytes 55304 | tf_op jit(solution)/shard_map/ppermute | solution.py:328
  25.5 5.4 %collective-permute-start.1 = (bf16[24,384]{1,0:T(8,128)(2,1)S(1)}, bf16[24,384]{1,0:T(8,128)(2,1)S(1)}, u32[]{:S(2)}, u32[]{:S(2)}) collective-permute-start(bf16[24,384]{1,0:T(8,128)(2,1)S(1)} %copy-done.12), channel_id=1, source_target_pairs={{0,128},{32,160},{64,192},{96,224},{128,0},{160,32},{192,64},{224,... | collective-permute-start | bytes 55304 | tf_op jit(solution)/shard_map/ppermute | solution.py:328
  30.9 2.7 %collective-permute-start.2 = (bf16[24,384]{1,0:T(8,128)(2,1)S(1)}, bf16[24,384]{1,0:T(8,128)(2,1)S(1)}, u32[]{:S(2)}, u32[]{:S(2)}) collective-permute-start(bf16[24,384]{1,0:T(8,128)(2,1)S(1)} %copy-done.12), channel_id=1, source_target_pairs={{0,192},{32,224},{64,0},{96,32},{128,64},{160,96},{192,128},{224,1... | collective-permute-start | bytes 55304 | tf_op jit(solution)/shard_map/ppermute | solution.py:328
  34.2 1.4 collective-permute-done.2
  38.5 2.9 %collective-permute-done.3 = bf16[96,384]{1,0:T(8,128)(2,1)S(1)} collective-permute-done((bf16[96,384]{1,0:T(8,128)(2,1)S(1)}, bf16[96,384]{1,0:T(8,128)(2,1)S(1)}, u32[]{:S(2)}, u32[]{:S(2)}) %collective-permute-start.3) | collective-permute-done | bytes 73760 | tf_op jit(solution)/shard_map/ppermute | solution.py:328
  42.1 1.6 %collective-permute-start.4 = (bf16[192,384]{1,0:T(8,128)(2,1)}, bf16[192,384]{1,0:T(8,128)(2,1)}, u32[]{:S(2)}, u32[]{:S(2)}) collective-permute-start(bf16[192,384]{1,0:T(8,128)(2,1)} %constant_dynamic-update-slice_fusion), channel_id=1, source_target_pairs={{0,8},{8,16},{16,24},{24,0},{1,9},{9,17},{17,25},{25,1},{2,10},{10... | collective-permute-start | bytes 442376 | tf_op jit(solution)/shard_map/ppermute | solution.py:328
  43.7 1.7 %collective-permute-start.5 = (bf16[192,384]{1,0:T(8,128)(2,1)}, bf16[192,384]{1,0:T(8,128)(2,1)}, u32[]{:S(2)}, u32[]{:S(2)}) collective-permute-start(bf16[192,384]{1,0:T(8,128)(2,1)} %constant_dynamic-update-slice_fusion), channel_id=1, source_target_pairs={{0,24},{8,0},{16,8},{24,16},{1,25},{9,1},{17,9},{25,17},{2,26},{10... | collective-permute-start | bytes 442376 | tf_op jit(solution)/shard_map/ppermute | solution.py:328
  45.3 1.7 %student.1.c0_ref = bf16[192,1280]{1,0:T(8,128)(2,1)S(1)} custom-call(s32[1,192]{1,0:T(1,128)S(1)} %copy-done.5, bf16[192,1280]{1,0:T(8,128)(2,1)S(1)} %copy-done, bf16[192,1280]{1,0:T(8,128)(2,1)S(1)} %copy-done.1, bf16[192,1280]{1,0:T(8,128)(2,1)S(1)} %copy-done.2), custom_call_target="tpu_custom_call" | custom-call | flops 1000000000 | bytes 2097152 | tf_op jit(solution)/shard_map/student/pallas_call | solution.py:168
  47.8 3.0 %pick.1 = bf16[1536,384]{1,0:T(8,128)(2,1)} custom-call(bf16[4,400,640]{2,1,0:T(8,128)(2,1)S(1)} %all-to-all-done.parts_ref), custom_call_target="tpu_custom_call" | custom-call | flops 1000000000 | bytes 4194304 | tf_op jit(solution)/shard_map/pick/pallas_call | solution.py:202
  50.8 11.0 %all-to-all-start.1 = ((bf16[64,24,384]{2,1,0:T(8,128)(2,1)}), bf16[64,24,384]{2,1,0:T(8,128)(2,1)S(1)}, u32[]{:S(2)}, u32[]{:S(2)}) async-start(bf16[64,24,384]{2,1,0:T(8,128)(2,1)} %bitcast.4), calls=%async_computation.1 | async-start | bytes 2359296 | tf_op jit(solution)/shard_map/all_to_all | solution.py:368
  61.9 2.0 %collective-permute-start.8 = (bf16[192,1280]{1,0:T(8,128)(2,1)S(1)}, bf16[192,1280]{1,0:T(8,128)(2,1)S(1)}, u32[]{:S(2)}, u32[]{:S(2)}) collective-permute-start(bf16[192,1280]{1,0:T(8,128)(2,1)S(1)} %copy-done.4), channel_id=1, source_target_pairs={{0,3},{1,0},{2,1},{3,2},{4,7},{5,4},{6,5},{7,6},{8,11},{9,8},{10,9... | collective-permute-start | bytes 1474568 | tf_op jit(solution)/shard_map/ppermute | solution.py:328
  64.9 1.6 %collective-permute-start.10 = (bf16[96,384]{1,0:T(8,128)(2,1)S(1)}, bf16[96,384]{1,0:T(8,128)(2,1)S(1)}, u32[]{:S(2)}, u32[]{:S(2)}) collective-permute-start(bf16[96,384]{1,0:T(8,128)(2,1)S(1)} %slice.17), channel_id=1, source_target_pairs={{0,8},{8,16},{16,24},{24,0},{1,9},{9,17},{17,25},{25,1},{2,10},{10... | collective-permute-start | bytes 221192 | tf_op jit(solution)/shard_map/ppermute | solution.py:328
  67.3 1.7 %collective-permute-start.11 = (bf16[96,384]{1,0:T(8,128)(2,1)S(1)}, bf16[96,384]{1,0:T(8,128)(2,1)S(1)}, u32[]{:S(2)}, u32[]{:S(2)}) collective-permute-start(bf16[96,384]{1,0:T(8,128)(2,1)S(1)} %slice.18), channel_id=1, source_target_pairs={{0,24},{8,0},{16,8},{24,16},{1,25},{9,1},{17,9},{25,17},{2,26},{10... | collective-permute-start | bytes 221192 | tf_op jit(solution)/shard_map/ppermute | solution.py:328
  73.0 2.1 %collective-permute-done.6.c1_ref = bf16[192,1280]{1,0:T(8,128)(2,1)S(1)} collective-permute-done((bf16[192,1280]{1,0:T(8,128)(2,1)S(1)}, bf16[192,1280]{1,0:T(8,128)(2,1)S(1)}, u32[]{:S(2)}, u32[]{:S(2)}) %collective-permute-start.6) | collective-permute-done | bytes 491552 | tf_op jit(solution)/shard_map/ppermute | solution.py:328
  75.5 2.7 %collective-permute-start.9 = (bf16[96,1280]{1,0:T(8,128)(2,1)S(1)}, bf16[96,1280]{1,0:T(8,128)(2,1)}, u32[]{:S(2)}, u32[]{:S(2)}) collective-permute-start(bf16[96,1280]{1,0:T(8,128)(2,1)S(1)} %slice.23), channel_id=1, source_target_pairs={{0,3},{1,0},{2,1},{3,2},{4,7},{5,4},{6,5},{7,6},{8,11},{9,8},{10,9... | collective-permute-start | bytes 737288 | tf_op jit(solution)/shard_map/ppermute | solution.py:328
  78.9 4.4 %collective-permute-done.7.c2_ref = bf16[96,1280]{1,0:T(8,128)(2,1)} collective-permute-done((bf16[96,1280]{1,0:T(8,128)(2,1)S(1)}, bf16[96,1280]{1,0:T(8,128)(2,1)}, u32[]{:S(2)}, u32[]{:S(2)}) %collective-permute-start.7) | collective-permute-done | bytes 245792 | tf_op jit(solution)/shard_map/ppermute | solution.py:328
  83.4 5.3 %project.1 = (f32[768,384]{1,0:T(8,128)}, bf16[1280,768]{1,0:T(8,128)(2,1)}, bf16[1280,384]{1,0:T(8,128)(2,1)}) custom-call(s32[3]{0:T(128)} %pad_add_fusion.2.at_ref, bf16[192,1280]{1,0:T(8,128)(2,1)} %copy-done.3, bf16[192,1280]{1,0:T(8,128)(2,1)} %copy-done.10, bf16[96,1280]{1,0:T(8,128)(2,1)} %collective-permute-done.7.c2_ref, ...), custom_call_target="tpu_custom_call" | custom-call | flops 1000000000 | bytes 8388608 | tf_op jit(solution)/shard_map/project/pallas_call | solution.py:241
  88.7 4.8 %all-to-all-done.1 = bf16[64,24,384]{2,1,0:T(8,128)(2,1)S(1)} async-done(((bf16[64,24,384]{2,1,0:T(8,128)(2,1)}), bf16[64,24,384]{2,1,0:T(8,128)(2,1)S(1)}, u32[]{:S(2)}, u32[]{:S(2)}) %all-to-all-start.1) | async-done | bytes 1179680 | tf_op jit(solution)/shard_map/all_to_all | solution.py:368
  93.5 1.5 %copy-done.7 = bf16[1280,768]{1,0:T(8,128)(2,1)S(1)} copy-done((bf16[1280,768]{1,0:T(8,128)(2,1)S(1)}, bf16[1280,768]{1,0:T(8,128)(2,1)}, u32[]{:S(2)}) %copy-start.7) | copy-done | bytes 1966104
  96.4 3.3 %land.1 = (bf16[768,384]{1,0:T(8,128)(2,1)S(1)}, bf16[768,384]{1,0:T(8,128)(2,1)S(1)}, f32[768,384]{1,0:T(8,128)S(1)}) custom-call(s32[2]{0:T(128)S(1)} %pad_add_fusion.1.place_ref, s32[1,1536]{1,0:T(1,128)S(1)} %copy-done.6, bf16[1536,384]{1,0:T(8,128)(2,1)S(1)} %bitcast.18, f32[768,384]{1,0:T(8,128)S(1)} %copy-done.8, bf16[1280,768]{1,0:T(8,128)(2,1)S(1)} %copy-done.7), custom_call_target="tpu_custom_call" | custom-call | flops 2000000000 | bytes 8388608 | tf_op jit(solution)/shard_map/land/pallas_call | solution.py:289
  99.8 1.5 %grad.1 = (f32[192,1280]{1,0:T(8,128)S(1)}, bf16[192,1280]{1,0:T(8,128)(2,1)S(1)}, bf16[192,1280]{1,0:T(8,128)(2,1)S(1)}, bf16[192,1280]{1,0:T(8,128)(2,1)S(1)}) custom-call(bf16[768,384]{1,0:T(8,128)(2,1)S(1)} %get-tuple-element.34.err_ref, bf16[1280,384]{1,0:T(8,128)(2,1)S(1)} %copy-done.9), custom_call_target="tpu_custom_call" | custom-call | flops 1000000000 | bytes 4194304 | tf_op jit(solution)/shard_map/grad/pallas_call | solution.py:314
  102.7 5.0 %all-to-all-start.2 = ((bf16[32,24,384]{2,1,0:T(8,128)(2,1)}), bf16[32,24,384]{2,1,0:T(8,128)(2,1)S(1)}, u32[]{:S(2)}, u32[]{:S(2)}) async-start(bf16[32,24,384]{2,1,0:T(8,128)(2,1)} %bitcast.19), calls=%async_computation.2 | async-start | bytes 1179648 | tf_op jit(solution)/shard_map/all_to_all | solution.py:384
  107.7 2.7 %collective-permute-start.16 = (bf16[192,1280]{1,0:T(8,128)(2,1)S(1)}, bf16[192,1280]{1,0:T(8,128)(2,1)S(1)}, u32[]{:S(2)}, u32[]{:S(2)}) collective-permute-start(bf16[192,1280]{1,0:T(8,128)(2,1)S(1)} %get-tuple-element.43), channel_id=1, source_target_pairs={{0,1},{1,2},{2,3},{3,0},{4,5},{5,6},{6,7},{7,4},{8,9},{9,10},{10,1... | collective-permute-start | bytes 1474568 | tf_op jit(solution)/shard_map/ppermute | solution.py:328
  110.5 2.5 %collective-permute-start.15 = (bf16[192,1280]{1,0:T(8,128)(2,1)S(1)}, bf16[192,1280]{1,0:T(8,128)(2,1)}, u32[]{:S(2)}, u32[]{:S(2)}) collective-permute-start(bf16[192,1280]{1,0:T(8,128)(2,1)S(1)} %get-tuple-element.42), channel_id=1, source_target_pairs={{0,2},{1,3},{2,0},{3,1},{4,6},{5,7},{6,4},{7,5},{8,10},{9,11},{10,... | collective-permute-start | bytes 1474568 | tf_op jit(solution)/shard_map/ppermute | solution.py:328
  113.0 2.5 %collective-permute-start.14 = (bf16[192,1280]{1,0:T(8,128)(2,1)S(1)}, bf16[192,1280]{1,0:T(8,128)(2,1)}, u32[]{:S(2)}, u32[]{:S(2)}) collective-permute-start(bf16[192,1280]{1,0:T(8,128)(2,1)S(1)} %get-tuple-element.41), channel_id=1, source_target_pairs={{0,3},{1,0},{2,1},{3,2},{4,7},{5,4},{6,5},{7,6},{8,11},{9,8},{10,9... | collective-permute-start | bytes 1474568 | tf_op jit(solution)/shard_map/ppermute | solution.py:328
  115.5 11.5 %all-to-all-done.2 = bf16[32,24,384]{2,1,0:T(8,128)(2,1)S(1)} async-done(((bf16[32,24,384]{2,1,0:T(8,128)(2,1)}), bf16[32,24,384]{2,1,0:T(8,128)(2,1)S(1)}, u32[]{:S(2)}, u32[]{:S(2)}) %all-to-all-start.2) | async-done | bytes 589856 | tf_op jit(solution)/shard_map/all_to_all | solution.py:384
  127.2 3.0 %collective-permute-start.19 = (f32[20,320]{1,0:T(8,128)S(1)}, f32[20,320]{1,0:T(8,128)S(1)}, u32[]{:S(2)}, u32[]{:S(2)}) collective-permute-start(f32[20,320]{1,0:T(8,128)S(1)} %get-tuple-element.47), channel_id=1, source_target_pairs={{0,3},{1,0},{2,1},{3,2},{4,7},{5,4},{6,5},{7,6},{8,11},{9,8},{10,9... | collective-permute-start | bytes 76808 | tf_op jit(solution)/shard_map/ppermute | solution.py:328
  130.2 2.2 %collective-permute-start.18 = (f32[20,320]{1,0:T(8,128)S(1)}, f32[20,320]{1,0:T(8,128)S(1)}, u32[]{:S(2)}, u32[]{:S(2)}) collective-permute-start(f32[20,320]{1,0:T(8,128)S(1)} %get-tuple-element.47), channel_id=1, source_target_pairs={{0,2},{1,3},{2,0},{3,1},{4,6},{5,7},{6,4},{7,5},{8,10},{9,11},{10,... | collective-permute-start | bytes 76808 | tf_op jit(solution)/shard_map/ppermute | solution.py:328
  132.4 2.5 %collective-permute-start.17 = (f32[20,320]{1,0:T(8,128)S(1)}, f32[20,320]{1,0:T(8,128)S(1)}, u32[]{:S(2)}, u32[]{:S(2)}) collective-permute-start(f32[20,320]{1,0:T(8,128)S(1)} %get-tuple-element.47), channel_id=1, source_target_pairs={{0,1},{1,2},{2,3},{3,0},{4,5},{5,6},{6,7},{7,4},{8,9},{9,10},{10,1... | collective-permute-start | bytes 76808 | tf_op jit(solution)/shard_map/ppermute | solution.py:328
  135.8 2.3 %add_add_fusion = f32[192,1280]{1,0:T(8,128)} fusion(f32[192,1280]{1,0:T(8,128)S(1)} %get-tuple-element.36, bf16[192,1280]{1,0:T(8,128)(2,1)S(1)} %collective-permute-done.16, bf16[192,1280]{1,0:T(8,128)(2,1)} %collective-permute-done.15, bf16[192,1280]{1,0:T(8,128)(2,1)} %collective-permute-done.14), kind=kLoop, calls=%fused_computation.3 | loop fusion | flops 1474560 | bytes 3440640 | tf_op jit(solution)/shard_map/add | solution.py:391
  (78 shorter events, 18.5 us)
Async XLA Ops:
  17.3 28.0 %copy-start = (bf16[192,1280]{1,0:T(8,128)(2,1)S(1)}, bf16[192,1280]{1,0:T(8,128)(2,1)}, u32[]{:S(2)}) copy-start(bf16[192,1280]{1,0:T(8,128)(2,1)} %q_ref.3) | copy-start | bytes 1474564
  17.3 28.0 %copy-start.1 = (bf16[192,1280]{1,0:T(8,128)(2,1)S(1)}, bf16[192,1280]{1,0:T(8,128)(2,1)}, u32[]{:S(2)}) copy-start(bf16[192,1280]{1,0:T(8,128)(2,1)} %k_ref.3) | copy-start | bytes 1474564
  17.3 28.0 %copy-start.2 = (bf16[192,1280]{1,0:T(8,128)(2,1)S(1)}, bf16[192,1280]{1,0:T(8,128)(2,1)}, u32[]{:S(2)}) copy-start(bf16[192,1280]{1,0:T(8,128)(2,1)} %v_ref.2) | copy-start | bytes 1474564
  17.4 28.0 %copy-start.5 = (s32[1,192]{1,0:T(1,128)S(1)}, s32[1,192]{1,0:T(1,128)}, u32[]{:S(2)}) copy-start(s32[1,192]{1,0:T(1,128)} %ids_ref.3) | copy-start | bytes 2308
  17.4 30.5 %all-to-all-start = ((bf16[4,400,640]{2,1,0:T(8,128)(2,1)}), bf16[4,400,640]{2,1,0:T(8,128)(2,1)S(1)}, u32[]{:S(2)}, u32[]{:S(2)}) async-start(bf16[4,400,640]{2,1,0:T(8,128)(2,1)} %get-tuple-element.24), calls=%async_computation | async-start | bytes 4096000 | tf_op jit(solution)/shard_map/all_to_all | solution.py:358
  23.3 10.9 %collective-permute-start = (bf16[24,384]{1,0:T(8,128)(2,1)S(1)}, bf16[24,384]{1,0:T(8,128)(2,1)S(1)}, u32[]{:S(2)}, u32[]{:S(2)}) collective-permute-start(bf16[24,384]{1,0:T(8,128)(2,1)S(1)} %copy-done.12), channel_id=1, source_target_pairs={{0,64},{32,96},{64,128},{96,160},{128,192},{160,224},{192,0},{224,... | collective-permute-start | bytes 55304 | tf_op jit(solution)/shard_map/ppermute | solution.py:328
  25.5 8.7 %collective-permute-start.1 = (bf16[24,384]{1,0:T(8,128)(2,1)S(1)}, bf16[24,384]{1,0:T(8,128)(2,1)S(1)}, u32[]{:S(2)}, u32[]{:S(2)}) collective-permute-start(bf16[24,384]{1,0:T(8,128)(2,1)S(1)} %copy-done.12), channel_id=1, source_target_pairs={{0,128},{32,160},{64,192},{96,224},{128,0},{160,32},{192,64},{224,... | collective-permute-start | bytes 55304 | tf_op jit(solution)/shard_map/ppermute | solution.py:328
  30.9 4.7 %collective-permute-start.2 = (bf16[24,384]{1,0:T(8,128)(2,1)S(1)}, bf16[24,384]{1,0:T(8,128)(2,1)S(1)}, u32[]{:S(2)}, u32[]{:S(2)}) collective-permute-start(bf16[24,384]{1,0:T(8,128)(2,1)S(1)} %copy-done.12), channel_id=1, source_target_pairs={{0,192},{32,224},{64,0},{96,32},{128,64},{160,96},{192,128},{224,1... | collective-permute-start | bytes 55304 | tf_op jit(solution)/shard_map/ppermute | solution.py:328
  35.6 5.8 %collective-permute-start.3 = (bf16[96,384]{1,0:T(8,128)(2,1)S(1)}, bf16[96,384]{1,0:T(8,128)(2,1)S(1)}, u32[]{:S(2)}, u32[]{:S(2)}) collective-permute-start(bf16[96,384]{1,0:T(8,128)(2,1)S(1)} %pad_maximum_fusion.1), channel_id=1, source_target_pairs={{0,32},{32,64},{64,96},{96,128},{128,160},{160,192},{192,224},{224... | collective-permute-start | bytes 221192 | tf_op jit(solution)/shard_map/ppermute | solution.py:328
  42.1 8.7 %collective-permute-start.4 = (bf16[192,384]{1,0:T(8,128)(2,1)}, bf16[192,384]{1,0:T(8,128)(2,1)}, u32[]{:S(2)}, u32[]{:S(2)}) collective-permute-start(bf16[192,384]{1,0:T(8,128)(2,1)} %constant_dynamic-update-slice_fusion), channel_id=1, source_target_pairs={{0,8},{8,16},{16,24},{24,0},{1,9},{9,17},{17,25},{25,1},{2,10},{10... | collective-permute-start | bytes 442376 | tf_op jit(solution)/shard_map/ppermute | solution.py:328
  43.7 7.1 %collective-permute-start.5 = (bf16[192,384]{1,0:T(8,128)(2,1)}, bf16[192,384]{1,0:T(8,128)(2,1)}, u32[]{:S(2)}, u32[]{:S(2)}) collective-permute-start(bf16[192,384]{1,0:T(8,128)(2,1)} %constant_dynamic-update-slice_fusion), channel_id=1, source_target_pairs={{0,24},{8,0},{16,8},{24,16},{1,25},{9,1},{17,9},{25,17},{2,26},{10... | collective-permute-start | bytes 442376 | tf_op jit(solution)/shard_map/ppermute | solution.py:328
  50.8 11.0 %copy-start.4 = (bf16[192,1280]{1,0:T(8,128)(2,1)S(1)}, bf16[192,1280]{1,0:T(8,128)(2,1)}, u32[]{:S(2)}) copy-start(bf16[192,1280]{1,0:T(8,128)(2,1)} %copy-done.3) | copy-start | bytes 1474564
  50.8 42.7 %all-to-all-start.1 = ((bf16[64,24,384]{2,1,0:T(8,128)(2,1)}), bf16[64,24,384]{2,1,0:T(8,128)(2,1)S(1)}, u32[]{:S(2)}, u32[]{:S(2)}) async-start(bf16[64,24,384]{2,1,0:T(8,128)(2,1)} %bitcast.4), calls=%async_computation.1 | async-start | bytes 2359296 | tf_op jit(solution)/shard_map/all_to_all | solution.py:368
  61.9 13.3 %collective-permute-start.6 = (bf16[192,1280]{1,0:T(8,128)(2,1)S(1)}, bf16[192,1280]{1,0:T(8,128)(2,1)S(1)}, u32[]{:S(2)}, u32[]{:S(2)}) collective-permute-start(bf16[192,1280]{1,0:T(8,128)(2,1)S(1)} %copy-done.4), channel_id=1, source_target_pairs={{0,1},{1,2},{2,3},{3,0},{4,5},{5,6},{6,7},{7,4},{8,9},{9,10},{10,1... | collective-permute-start | bytes 1474568 | tf_op jit(solution)/shard_map/ppermute | solution.py:328
  61.9 13.6 %collective-permute-start.8 = (bf16[192,1280]{1,0:T(8,128)(2,1)S(1)}, bf16[192,1280]{1,0:T(8,128)(2,1)S(1)}, u32[]{:S(2)}, u32[]{:S(2)}) collective-permute-start(bf16[192,1280]{1,0:T(8,128)(2,1)S(1)} %copy-done.4), channel_id=1, source_target_pairs={{0,3},{1,0},{2,1},{3,2},{4,7},{5,4},{6,5},{7,6},{8,11},{9,8},{10,9... | collective-permute-start | bytes 1474568 | tf_op jit(solution)/shard_map/ppermute | solution.py:328
  64.9 6.7 %collective-permute-start.10 = (bf16[96,384]{1,0:T(8,128)(2,1)S(1)}, bf16[96,384]{1,0:T(8,128)(2,1)S(1)}, u32[]{:S(2)}, u32[]{:S(2)}) collective-permute-start(bf16[96,384]{1,0:T(8,128)(2,1)S(1)} %slice.17), channel_id=1, source_target_pairs={{0,8},{8,16},{16,24},{24,0},{1,9},{9,17},{17,25},{25,1},{2,10},{10... | collective-permute-start | bytes 221192 | tf_op jit(solution)/shard_map/ppermute | solution.py:328
  67.3 4.7 %collective-permute-start.11 = (bf16[96,384]{1,0:T(8,128)(2,1)S(1)}, bf16[96,384]{1,0:T(8,128)(2,1)S(1)}, u32[]{:S(2)}, u32[]{:S(2)}) collective-permute-start(bf16[96,384]{1,0:T(8,128)(2,1)S(1)} %slice.18), channel_id=1, source_target_pairs={{0,24},{8,0},{16,8},{24,16},{1,25},{9,1},{17,9},{25,17},{2,26},{10... | collective-permute-start | bytes 221192 | tf_op jit(solution)/shard_map/ppermute | solution.py:328
  72.9 10.4 %copy-start.13 = (bf16[768,384]{1,0:T(8,128)(2,1)}, bf16[768,384]{1,0:T(8,128)(2,1)S(1)}, u32[]{:S(2)}) copy-start(bf16[768,384]{1,0:T(8,128)(2,1)S(1)} %constant_dynamic-update-slice_fusion.5.near_ref) | copy-start | bytes 1769476
  72.9 6.0 %collective-permute-start.12 = (bf16[768,384]{1,0:T(8,128)(2,1)S(1)}, bf16[768,384]{1,0:T(8,128)(2,1)}, u32[]{:S(2)}, u32[]{:S(2)}) collective-permute-start(bf16[768,384]{1,0:T(8,128)(2,1)S(1)} %constant_dynamic-update-slice_fusion.5.near_ref), channel_id=1, source_target_pairs={{0,4},{4,0},{1,5},{5,1},{2,6},{6,2},{3,7},{7,3},{8,12},{12,8},{9,1... | collective-permute-start | bytes 1769480 | tf_op jit(solution)/shard_map/ppermute | solution.py:328
  75.1 8.2 %copy-start.10 = (bf16[192,1280]{1,0:T(8,128)(2,1)}, bf16[192,1280]{1,0:T(8,128)(2,1)S(1)}, u32[]{:S(2)}) copy-start(bf16[192,1280]{1,0:T(8,128)(2,1)S(1)} %collective-permute-done.6.c1_ref) | copy-start | bytes 1474564
  75.1 8.2 %collective-permute-start.7 = (bf16[96,1280]{1,0:T(8,128)(2,1)S(1)}, bf16[96,1280]{1,0:T(8,128)(2,1)}, u32[]{:S(2)}, u32[]{:S(2)}) collective-permute-start(bf16[96,1280]{1,0:T(8,128)(2,1)S(1)} %slice.22), channel_id=1, source_target_pairs={{0,1},{1,2},{2,3},{3,0},{4,5},{5,6},{6,7},{7,4},{8,9},{9,10},{10,1... | collective-permute-start | bytes 737288 | tf_op jit(solution)/shard_map/ppermute | solution.py:328
  75.5 7.8 %copy-start.11 = (bf16[192,1280]{1,0:T(8,128)(2,1)}, bf16[192,1280]{1,0:T(8,128)(2,1)S(1)}, u32[]{:S(2)}) copy-start(bf16[192,1280]{1,0:T(8,128)(2,1)S(1)} %collective-permute-done.8.c4_ref) | copy-start | bytes 1474564
  75.5 7.8 %collective-permute-start.9 = (bf16[96,1280]{1,0:T(8,128)(2,1)S(1)}, bf16[96,1280]{1,0:T(8,128)(2,1)}, u32[]{:S(2)}, u32[]{:S(2)}) collective-permute-start(bf16[96,1280]{1,0:T(8,128)(2,1)S(1)} %slice.23), channel_id=1, source_target_pairs={{0,3},{1,0},{2,1},{3,2},{4,7},{5,4},{6,5},{7,6},{8,11},{9,8},{10,9... | collective-permute-start | bytes 737288 | tf_op jit(solution)/shard_map/ppermute | solution.py:328
  78.9 14.6 %copy-start.6 = (s32[1,1536]{1,0:T(1,128)S(1)}, s32[1,1536]{1,0:T(1,128)}, u32[]{:S(2)}) copy-start(s32[1,1536]{1,0:T(1,128)} %constant.42.clone.t_ref) | copy-start | bytes 18436
  99.6 2.1 %collective-permute-start.13 = (bf16[768,384]{1,0:T(8,128)(2,1)S(1)}, bf16[768,384]{1,0:T(8,128)(2,1)S(1)}, u32[]{:S(2)}, u32[]{:S(2)}) collective-permute-start(bf16[768,384]{1,0:T(8,128)(2,1)S(1)} %get-tuple-element.37), channel_id=1, source_target_pairs={{0,4},{4,0},{1,5},{5,1},{2,6},{6,2},{3,7},{7,3},{8,12},{12,8},{9,1... | collective-permute-start | bytes 1769480 | tf_op jit(solution)/shard_map/ppermute | solution.py:328
  102.7 24.4 %all-to-all-start.2 = ((bf16[32,24,384]{2,1,0:T(8,128)(2,1)}), bf16[32,24,384]{2,1,0:T(8,128)(2,1)S(1)}, u32[]{:S(2)}, u32[]{:S(2)}) async-start(bf16[32,24,384]{2,1,0:T(8,128)(2,1)} %bitcast.19), calls=%async_computation.2 | async-start | bytes 1179648 | tf_op jit(solution)/shard_map/all_to_all | solution.py:384
  107.7 24.7 %collective-permute-start.16 = (bf16[192,1280]{1,0:T(8,128)(2,1)S(1)}, bf16[192,1280]{1,0:T(8,128)(2,1)S(1)}, u32[]{:S(2)}, u32[]{:S(2)}) collective-permute-start(bf16[192,1280]{1,0:T(8,128)(2,1)S(1)} %get-tuple-element.43), channel_id=1, source_target_pairs={{0,1},{1,2},{2,3},{3,0},{4,5},{5,6},{6,7},{7,4},{8,9},{9,10},{10,1... | collective-permute-start | bytes 1474568 | tf_op jit(solution)/shard_map/ppermute | solution.py:328
  110.5 24.5 %collective-permute-start.15 = (bf16[192,1280]{1,0:T(8,128)(2,1)S(1)}, bf16[192,1280]{1,0:T(8,128)(2,1)}, u32[]{:S(2)}, u32[]{:S(2)}) collective-permute-start(bf16[192,1280]{1,0:T(8,128)(2,1)S(1)} %get-tuple-element.42), channel_id=1, source_target_pairs={{0,2},{1,3},{2,0},{3,1},{4,6},{5,7},{6,4},{7,5},{8,10},{9,11},{10,... | collective-permute-start | bytes 1474568 | tf_op jit(solution)/shard_map/ppermute | solution.py:328
  113.0 22.8 %collective-permute-start.14 = (bf16[192,1280]{1,0:T(8,128)(2,1)S(1)}, bf16[192,1280]{1,0:T(8,128)(2,1)}, u32[]{:S(2)}, u32[]{:S(2)}) collective-permute-start(bf16[192,1280]{1,0:T(8,128)(2,1)S(1)} %get-tuple-element.41), channel_id=1, source_target_pairs={{0,3},{1,0},{2,1},{3,2},{4,7},{5,4},{6,5},{7,6},{8,11},{9,8},{10,9... | collective-permute-start | bytes 1474568 | tf_op jit(solution)/shard_map/ppermute | solution.py:328
  127.2 10.9 %collective-permute-start.19 = (f32[20,320]{1,0:T(8,128)S(1)}, f32[20,320]{1,0:T(8,128)S(1)}, u32[]{:S(2)}, u32[]{:S(2)}) collective-permute-start(f32[20,320]{1,0:T(8,128)S(1)} %get-tuple-element.47), channel_id=1, source_target_pairs={{0,3},{1,0},{2,1},{3,2},{4,7},{5,4},{6,5},{7,6},{8,11},{9,8},{10,9... | collective-permute-start | bytes 76808 | tf_op jit(solution)/shard_map/ppermute | solution.py:328
  130.2 7.9 %collective-permute-start.18 = (f32[20,320]{1,0:T(8,128)S(1)}, f32[20,320]{1,0:T(8,128)S(1)}, u32[]{:S(2)}, u32[]{:S(2)}) collective-permute-start(f32[20,320]{1,0:T(8,128)S(1)} %get-tuple-element.47), channel_id=1, source_target_pairs={{0,2},{1,3},{2,0},{3,1},{4,6},{5,7},{6,4},{7,5},{8,10},{9,11},{10,... | collective-permute-start | bytes 76808 | tf_op jit(solution)/shard_map/ppermute | solution.py:328
  132.4 5.7 %collective-permute-start.17 = (f32[20,320]{1,0:T(8,128)S(1)}, f32[20,320]{1,0:T(8,128)S(1)}, u32[]{:S(2)}, u32[]{:S(2)}) collective-permute-start(f32[20,320]{1,0:T(8,128)S(1)} %get-tuple-element.47), channel_id=1, source_target_pairs={{0,1},{1,2},{2,3},{3,0},{4,5},{5,6},{6,7},{7,4},{8,9},{9,10},{10,1... | collective-permute-start | bytes 76808 | tf_op jit(solution)/shard_map/ppermute | solution.py:328
  (5 other events, 13.0 us)

commit v3 on v2

--- a/solution.py
+++ b/solution.py
@@ -54,7 +54,7 @@
     return jnp.concatenate([table, jnp.zeros((TABLE, wide - n), F32)], axis=1).astype(BF)
 
 
-def teacher_kernel(x_ref, ids_ref, sends_ref, w_ref, q_ref, k_ref, v_ref, map_hbm, out_ref, mine_ref, qx, kx, ve, ctx,
+def teacher_kernel(x_ref, ids_ref, owner_ref, slot_ref, w_ref, q_ref, k_ref, v_ref, map_hbm, out_ref, mine_ref, qx, kx, ve, ctx,
                    map_ref, sem):
     step = pl.program_id(0)
     fetch = pltpu.make_async_copy(map_hbm, map_ref, sem)
@@ -68,8 +68,8 @@
         hot, far = segment_columns(ids_ref[...])
         qx[...] = hot
         kx[...] = far
-        ve[:, HDT:] = jnp.ones((rows, HDT), BF)
-        table = send_table(sends_ref[0:1, :], sends_ref[1:2, :], out_ref.shape[2])
+        ve[:, :, HDT:] = jnp.ones((2, rows, HDT), BF)
+        table = send_table(owner_ref[...].reshape(1, -1), slot_ref[...].reshape(1, -1), out_ref.shape[2])
         for n in range(4):
             out_ref[n, half:, :] = table
         weight = w_ref[...].astype(F32)
@@ -85,12 +85,12 @@
     for h in range(2):
         cols = slice(h * HDT, (h + 1) * HDT)
         ke = jnp.concatenate([k_ref[:, cols], kx[...]], axis=1)
-        ve[:, :HDT] = v_ref[:, cols]
+        ve[h, :, :HDT] = v_ref[:, cols]
         for r in range(0, rows, 256):
             qe = jnp.concatenate([q_ref[r:r + 256, cols], qx[r:r + 256, :]], axis=1)
             s = lax.dot_general(qe, ke, NT, preferred_element_type=F32)
             p = softmax_rows(s, scale)
-            o = jnp.dot(p, ve[...], preferred_element_type=F32)
+            o = jnp.dot(p, ve[h], preferred_element_type=F32)
             c = (o[:, :HDT] / o[:, HDT:]).astype(BF)
             ctx[r:r + 256, pl.ds(pl.multiple_of(step * 256 + h * HDT, HDT), HDT)] = c
 
@@ -107,7 +107,7 @@
                 ).astype(BF)
 
 
-def teacher(x, ids, sends, weight, q, k, v, tmap):
+def teacher(x, ids, owner, slot, weight, q, k, v, tmap):
     rows, width = q.shape
     out = tmap.shape[1]
     half = rows // 2
@@ -121,7 +121,8 @@
         in_specs=[
             pl.BlockSpec(memory_space=pltpu.SMEM),
             pl.BlockSpec((1, rows), lambda i: (0, 0)),
-            pl.BlockSpec(sends.shape, lambda i: (0, 0)),
+            pl.BlockSpec(owner.shape, lambda i: (0,)),
+            pl.BlockSpec(slot.shape, lambda i: (0,)),
             pl.BlockSpec(weight.shape, lambda i: (0, 0)),
             pl.BlockSpec((rows, pair), lambda i: (0, i)),
             pl.BlockSpec((rows, pair), lambda i: (0, i)),
@@ -133,7 +134,7 @@
         scratch_shapes=[
             pltpu.VMEM((rows, 128), BF),
             pltpu.VMEM((rows, 128), BF),
-            pltpu.VMEM((rows, pair), BF),
+            pltpu.VMEM((2, rows, pair), BF),
             pltpu.VMEM((rows, width), BF),
             pltpu.VMEM((width, out), BF),
             pltpu.SemaphoreType.DMA,
@@ -141,7 +142,7 @@
         compiler_params=params(60),
         cost_estimate=pl.CostEstimate(flops=10 * 10**9, bytes_accessed=10 * 2**20, transcendentals=6 * 10**6),
         name="teacher",
-    )(x, ids, sends, weight, q, k, v, tmap)
+    )(x, ids, owner, slot, weight, q, k, v, tmap)
 
 
 def student_kernel(ids_ref, q_ref, k_ref, v_ref, o_ref):
@@ -174,6 +175,15 @@
     )(ids, q, k, v)
 
 
+def one_hot(row, index, start):
+    near = jnp.minimum(jnp.maximum(index - start, -1.0), 256.0).astype(BF)
+    return jnp.where(row == near, jnp.ones_like(row), jnp.zeros_like(row))
+
+
+def count_rows(n):
+    return lax.broadcasted_iota(jnp.int32, (256, n), 0).astype(F32).astype(BF)
+
+
 def select_kernel(capacity, unit, parts_ref, o_ref, rows_ref):
     half = parts_ref.shape[1] - TABLE
     block = parts_ref.shape[2] // 2
@@ -181,7 +191,7 @@
     table = [parts_ref[n, half:, :quarter].astype(F32) for n in range(4)]
     idx = jnp.concatenate(
         [t[0:1, :] * unit + t[1:2, :] + n * capacity for n, t in enumerate(table)], axis=1
-    ).astype(jnp.int32)
+    )
     slot = jnp.concatenate([t[2:3, :] for t in table], axis=1)
     mark = jnp.transpose(jnp.broadcast_to(slot + 1.0, (128, 2 * half)))[:, :WIDE - block]
     for r in (0, quarter):
@@ -191,9 +201,9 @@
             rows_ref[m:m + quarter, :] = jnp.concatenate(
                 [total[:, c:c + block], mark[m:m + quarter, :]], axis=1
             ).astype(BF)
+    row = count_rows(2 * half)
     for r in range(0, o_ref.shape[0], 256):
-        row = lax.broadcasted_iota(jnp.int32, (256, 2 * half), 0) + r
-        hot = (row == idx).astype(F32).astype(BF)
+        hot = one_hot(row, idx, float(r))
         o_ref[r:r + 256, :] = jnp.dot(hot, rows_ref[...], preferred_element_type=F32).astype(BF)
 
 
@@ -263,11 +273,11 @@
     block = WIDE - 64
     slot = jnp.transpose(arrived_ref[:, 256:].astype(F32))[64:65, :].astype(jnp.int32)
     base = jnp.bitwise_and(place_ref[0] + 4 - t_ref[...], 3) * quarter - 1
-    dst = jnp.where(slot > 0, slot + base, -1)
+    dst = jnp.where(slot > 0, slot + base, -1).astype(F32)
+    row = count_rows(dst.shape[1])
     valid = lax.broadcasted_iota(jnp.int32, (256, WIDE), 1) < block
     for r in range(0, rows, 256):
-        row = lax.broadcasted_iota(jnp.int32, (256, dst.shape[1]), 0) + r
-        hot = (row == dst).astype(F32).astype(BF)
+        hot = one_hot(row, dst, float(r))
         target = jnp.dot(hot, arrived_ref[...], preferred_element_type=F32)
         err_ref[r:r + 256, :] = jnp.where(valid, pred_ref[r:r + 256, :] - target, 0.0).astype(BF)
     n = ctxt_ref.shape[0] // (2 * unit)
@@ -353,8 +363,7 @@
     own_rows = s_weight.shape[0]
     padded = own_rows + -own_rows % 8
 
-    sends = jnp.stack([send_owner, send_slot])
-    parts, mine = teacher(xs, t_segments, sends, s_weight, t_query, t_key, t_value, teacher_map)
+    parts, mine = teacher(xs, t_segments, send_owner, send_slot, s_weight, t_query, t_key, t_value, teacher_map)
     parts = lax.all_to_all(parts, "tensor", 0, 0, tiled=True)
     outgoing = select(parts, owners, capacity)
 

time: 142 us -> 140 us (0.986)
  no operation moved by 1% of the time
where the time goes in v3:
time: 140 us; the launch traced here: 138 us
  starting transfers between devices  60.7 us (43%)
  Pallas kernels  30.1 us (22%)
  waiting for transfers between devices  29.6 us (21%)
  local copies, waits for them, and re-layouts  12.7 us (9%)
  other arithmetic  4.18 us (3%)
    ppermute x20, starting transfers between devices, go(): return lax.ppermute(a, axis, ring(lax.axis_size(axis), k))  38.8 us
    pallas_call x1, Pallas kernels, teacher(): pl.pallas_call(teacher_kernel, grid=(steps,), in_specs=[pl.BlockSpec(memo...  15.3 us
    ppermute x20, waiting for transfers between devices, go(): return lax.ppermute(a, axis, ring(lax.axis_size(axis), k))  13.2 us
    all_to_all x1, waiting for transfers between devices, local(): terms = lax.all_to_all(term, ('z', 'y'), 0, 0, tiled=True)  11.5 us
    all_to_all x1, starting transfers between devices, local(): arrived = lax.all_to_all(outgoing, DP, 0, 0, tiled=True)  11 us
    unnamed x36, local copies, waits for them, and re-layouts  7.99 us
    all_to_all x1, starting transfers between devices, local(): parts = lax.all_to_all(parts, 'tensor', 0, 0, tiled=True)  5.93 us
    pallas_call x1, Pallas kernels, project(): pl.pallas_call(functools.partial(project_kernel, unit, padded), in_specs=...  5.34 us
  transfers between devices with their start and end apart: 23, of which 10 were waited for; matrix products, arithmetic and copies ran while one was open for 8% of the time, Pallas kernels for 8%

profile of v3, /device:TPU:2, one launch (start us, length us, event | category | flops | bytes accessed | tf_op | source)
XLA Modules:
  0.0 138.2 jit_solution(4151501805895635003)
XLA Ops:
  0.6 15.3 %teacher.1 = (bf16[4,400,640]{2,1,0:T(8,128)(2,1)}, bf16[24,384]{1,0:T(8,128)(2,1)}) custom-call(s32[1]{0:T(128)} %bitcast.x_ref, s32[1,768]{1,0:T(1,128)} %ids_ref.2, s32[192]{0:T(256)} %owner_ref.1, s32[192]{0:T(256)} %slot_ref.1, bf16[20,1280]{1,0:T(8,128)(2,1)} %w_ref.1, bf16[768,1280]{1,0:T(8,128)(2,1)} %q_ref.2, bf16[768,1280]{1,0:T(8,128)(2,1)} %k_ref.2, ...), custom_call_target="tpu_custom_call" | custom-call | flops 10000000000 | bytes 10485760 | tf_op jit(solution)/shard_map/teacher/pallas_call | solution.py:118
  16.0 5.9 %all-to-all-start = ((bf16[4,400,640]{2,1,0:T(8,128)(2,1)}), bf16[4,400,640]{2,1,0:T(8,128)(2,1)S(1)}, u32[]{:S(2)}, u32[]{:S(2)}) async-start(bf16[4,400,640]{2,1,0:T(8,128)(2,1)} %get-tuple-element.24), calls=%async_computation | async-start | bytes 4096000 | tf_op jit(solution)/shard_map/all_to_all | solution.py:367
  22.0 2.3 %collective-permute-start = (bf16[24,384]{1,0:T(8,128)(2,1)S(1)}, bf16[24,384]{1,0:T(8,128)(2,1)S(1)}, u32[]{:S(2)}, u32[]{:S(2)}) collective-permute-start(bf16[24,384]{1,0:T(8,128)(2,1)S(1)} %copy-done.12), channel_id=1, source_target_pairs={{0,64},{32,96},{64,128},{96,160},{128,192},{160,224},{192,0},{224,... | collective-permute-start | bytes 55304 | tf_op jit(solution)/shard_map/ppermute | solution.py:338
  24.2 5.4 %collective-permute-start.1 = (bf16[24,384]{1,0:T(8,128)(2,1)S(1)}, bf16[24,384]{1,0:T(8,128)(2,1)S(1)}, u32[]{:S(2)}, u32[]{:S(2)}) collective-permute-start(bf16[24,384]{1,0:T(8,128)(2,1)S(1)} %copy-done.12), channel_id=1, source_target_pairs={{0,128},{32,160},{64,192},{96,224},{128,0},{160,32},{192,64},{224,... | collective-permute-start | bytes 55304 | tf_op jit(solution)/shard_map/ppermute | solution.py:338
  29.6 2.7 %collective-permute-start.2 = (bf16[24,384]{1,0:T(8,128)(2,1)S(1)}, bf16[24,384]{1,0:T(8,128)(2,1)S(1)}, u32[]{:S(2)}, u32[]{:S(2)}) collective-permute-start(bf16[24,384]{1,0:T(8,128)(2,1)S(1)} %copy-done.12), channel_id=1, source_target_pairs={{0,192},{32,224},{64,0},{96,32},{128,64},{160,96},{192,128},{224,1... | collective-permute-start | bytes 55304 | tf_op jit(solution)/shard_map/ppermute | solution.py:338
  32.9 1.4 collective-permute-done.2
  37.2 2.9 %collective-permute-done.3 = bf16[96,384]{1,0:T(8,128)(2,1)S(1)} collective-permute-done((bf16[96,384]{1,0:T(8,128)(2,1)S(1)}, bf16[96,384]{1,0:T(8,128)(2,1)S(1)}, u32[]{:S(2)}, u32[]{:S(2)}) %collective-permute-start.3) | collective-permute-done | bytes 73760 | tf_op jit(solution)/shard_map/ppermute | solution.py:338
  40.8 1.6 %collective-permute-start.4 = (bf16[192,384]{1,0:T(8,128)(2,1)}, bf16[192,384]{1,0:T(8,128)(2,1)}, u32[]{:S(2)}, u32[]{:S(2)}) collective-permute-start(bf16[192,384]{1,0:T(8,128)(2,1)} %constant_dynamic-update-slice_fusion), channel_id=1, source_target_pairs={{0,8},{8,16},{16,24},{24,0},{1,9},{9,17},{17,25},{25,1},{2,10},{10... | collective-permute-start | bytes 442376 | tf_op jit(solution)/shard_map/ppermute | solution.py:338
  42.3 1.7 %collective-permute-start.5 = (bf16[192,384]{1,0:T(8,128)(2,1)}, bf16[192,384]{1,0:T(8,128)(2,1)}, u32[]{:S(2)}, u32[]{:S(2)}) collective-permute-start(bf16[192,384]{1,0:T(8,128)(2,1)} %constant_dynamic-update-slice_fusion), channel_id=1, source_target_pairs={{0,24},{8,0},{16,8},{24,16},{1,25},{9,1},{17,9},{25,17},{2,26},{10... | collective-permute-start | bytes 442376 | tf_op jit(solution)/shard_map/ppermute | solution.py:338
  44.0 1.7 %student.1.c0_ref = bf16[192,1280]{1,0:T(8,128)(2,1)S(1)} custom-call(s32[1,192]{1,0:T(1,128)S(1)} %copy-done.5, bf16[192,1280]{1,0:T(8,128)(2,1)S(1)} %copy-done, bf16[192,1280]{1,0:T(8,128)(2,1)S(1)} %copy-done.1, bf16[192,1280]{1,0:T(8,128)(2,1)S(1)} %copy-done.2), custom_call_target="tpu_custom_call" | custom-call | flops 1000000000 | bytes 2097152 | tf_op jit(solution)/shard_map/student/pallas_call | solution.py:169
  46.5 2.9 %pick.1 = bf16[1536,384]{1,0:T(8,128)(2,1)} custom-call(bf16[4,400,640]{2,1,0:T(8,128)(2,1)S(1)} %all-to-all-done.parts_ref), custom_call_target="tpu_custom_call" | custom-call | flops 1000000000 | bytes 4194304 | tf_op jit(solution)/shard_map/pick/pallas_call | solution.py:212
  49.5 11.0 %all-to-all-start.1 = ((bf16[64,24,384]{2,1,0:T(8,128)(2,1)}), bf16[64,24,384]{2,1,0:T(8,128)(2,1)S(1)}, u32[]{:S(2)}, u32[]{:S(2)}) async-start(bf16[64,24,384]{2,1,0:T(8,128)(2,1)} %bitcast.2), calls=%async_computation.1 | async-start | bytes 2359296 | tf_op jit(solution)/shard_map/all_to_all | solution.py:377
  60.6 2.0 %collective-permute-start.8 = (bf16[192,1280]{1,0:T(8,128)(2,1)S(1)}, bf16[192,1280]{1,0:T(8,128)(2,1)S(1)}, u32[]{:S(2)}, u32[]{:S(2)}) collective-permute-start(bf16[192,1280]{1,0:T(8,128)(2,1)S(1)} %copy-done.4), channel_id=1, source_target_pairs={{0,3},{1,0},{2,1},{3,2},{4,7},{5,4},{6,5},{7,6},{8,11},{9,8},{10,9... | collective-permute-start | bytes 1474568 | tf_op jit(solution)/shard_map/ppermute | solution.py:338
  63.5 1.6 %collective-permute-start.10 = (bf16[96,384]{1,0:T(8,128)(2,1)S(1)}, bf16[96,384]{1,0:T(8,128)(2,1)S(1)}, u32[]{:S(2)}, u32[]{:S(2)}) collective-permute-start(bf16[96,384]{1,0:T(8,128)(2,1)S(1)} %slice.17), channel_id=1, source_target_pairs={{0,8},{8,16},{16,24},{24,0},{1,9},{9,17},{17,25},{25,1},{2,10},{10... | collective-permute-start | bytes 221192 | tf_op jit(solution)/shard_map/ppermute | solution.py:338
  66.0 1.7 %collective-permute-start.11 = (bf16[96,384]{1,0:T(8,128)(2,1)S(1)}, bf16[96,384]{1,0:T(8,128)(2,1)S(1)}, u32[]{:S(2)}, u32[]{:S(2)}) collective-permute-start(bf16[96,384]{1,0:T(8,128)(2,1)S(1)} %slice.18), channel_id=1, source_target_pairs={{0,24},{8,0},{16,8},{24,16},{1,25},{9,1},{17,9},{25,17},{2,26},{10... | collective-permute-start | bytes 221192 | tf_op jit(solution)/shard_map/ppermute | solution.py:338
  71.7 2.1 %collective-permute-done.6.c1_ref = bf16[192,1280]{1,0:T(8,128)(2,1)S(1)} collective-permute-done((bf16[192,1280]{1,0:T(8,128)(2,1)S(1)}, bf16[192,1280]{1,0:T(8,128)(2,1)S(1)}, u32[]{:S(2)}, u32[]{:S(2)}) %collective-permute-start.6) | collective-permute-done | bytes 491552 | tf_op jit(solution)/shard_map/ppermute | solution.py:338
  74.2 2.7 %collective-permute-start.9 = (bf16[96,1280]{1,0:T(8,128)(2,1)S(1)}, bf16[96,1280]{1,0:T(8,128)(2,1)}, u32[]{:S(2)}, u32[]{:S(2)}) collective-permute-start(bf16[96,1280]{1,0:T(8,128)(2,1)S(1)} %slice.23), channel_id=1, source_target_pairs={{0,3},{1,0},{2,1},{3,2},{4,7},{5,4},{6,5},{7,6},{8,11},{9,8},{10,9... | collective-permute-start | bytes 737288 | tf_op jit(solution)/shard_map/ppermute | solution.py:338
  77.6 4.4 %collective-permute-done.7.c2_ref = bf16[96,1280]{1,0:T(8,128)(2,1)} collective-permute-done((bf16[96,1280]{1,0:T(8,128)(2,1)S(1)}, bf16[96,1280]{1,0:T(8,128)(2,1)}, u32[]{:S(2)}, u32[]{:S(2)}) %collective-permute-start.7) | collective-permute-done | bytes 245792 | tf_op jit(solution)/shard_map/ppermute | solution.py:338
  82.0 5.3 %project.1 = (f32[768,384]{1,0:T(8,128)}, bf16[1280,768]{1,0:T(8,128)(2,1)}, bf16[1280,384]{1,0:T(8,128)(2,1)}) custom-call(s32[3]{0:T(128)} %pad_add_fusion.1.at_ref, bf16[192,1280]{1,0:T(8,128)(2,1)} %copy-done.3, bf16[192,1280]{1,0:T(8,128)(2,1)} %copy-done.10, bf16[96,1280]{1,0:T(8,128)(2,1)} %collective-permute-done.7.c2_ref, ...), custom_call_target="tpu_custom_call" | custom-call | flops 1000000000 | bytes 8388608 | tf_op jit(solution)/shard_map/project/pallas_call | solution.py:251
  87.3 4.9 %all-to-all-done.1 = bf16[64,24,384]{2,1,0:T(8,128)(2,1)S(1)} async-done(((bf16[64,24,384]{2,1,0:T(8,128)(2,1)}), bf16[64,24,384]{2,1,0:T(8,128)(2,1)S(1)}, u32[]{:S(2)}, u32[]{:S(2)}) %all-to-all-start.1) | async-done | bytes 1179680 | tf_op jit(solution)/shard_map/all_to_all | solution.py:377
  92.2 1.5 %copy-done.7 = bf16[1280,768]{1,0:T(8,128)(2,1)S(1)} copy-done((bf16[1280,768]{1,0:T(8,128)(2,1)S(1)}, bf16[1280,768]{1,0:T(8,128)(2,1)}, u32[]{:S(2)}) %copy-start.7) | copy-done | bytes 1966104
  95.0 3.3 %land.1 = (bf16[768,384]{1,0:T(8,128)(2,1)S(1)}, bf16[768,384]{1,0:T(8,128)(2,1)S(1)}, f32[768,384]{1,0:T(8,128)S(1)}) custom-call(s32[2]{0:T(128)S(1)} %pad_add_fusion.place_ref, s32[1,1536]{1,0:T(1,128)S(1)} %copy-done.6, bf16[1536,384]{1,0:T(8,128)(2,1)S(1)} %bitcast.16, f32[768,384]{1,0:T(8,128)S(1)} %copy-done.8, bf16[1280,768]{1,0:T(8,128)(2,1)S(1)} %copy-done.7), custom_call_target="tpu_custom_call" | custom-call | flops 2000000000 | bytes 8388608 | tf_op jit(solution)/shard_map/land/pallas_call | solution.py:299
  98.4 1.5 %grad.1 = (f32[192,1280]{1,0:T(8,128)S(1)}, bf16[192,1280]{1,0:T(8,128)(2,1)S(1)}, bf16[192,1280]{1,0:T(8,128)(2,1)S(1)}, bf16[192,1280]{1,0:T(8,128)(2,1)S(1)}) custom-call(bf16[768,384]{1,0:T(8,128)(2,1)S(1)} %get-tuple-element.34.err_ref, bf16[1280,384]{1,0:T(8,128)(2,1)S(1)} %copy-done.9), custom_call_target="tpu_custom_call" | custom-call | flops 1000000000 | bytes 4194304 | tf_op jit(solution)/shard_map/grad/pallas_call | solution.py:324
  101.3 5.0 %all-to-all-start.2 = ((bf16[32,24,384]{2,1,0:T(8,128)(2,1)}), bf16[32,24,384]{2,1,0:T(8,128)(2,1)S(1)}, u32[]{:S(2)}, u32[]{:S(2)}) async-start(bf16[32,24,384]{2,1,0:T(8,128)(2,1)} %bitcast.17), calls=%async_computation.2 | async-start | bytes 1179648 | tf_op jit(solution)/shard_map/all_to_all | solution.py:393
  106.3 2.7 %collective-permute-start.16 = (bf16[192,1280]{1,0:T(8,128)(2,1)S(1)}, bf16[192,1280]{1,0:T(8,128)(2,1)S(1)}, u32[]{:S(2)}, u32[]{:S(2)}) collective-permute-start(bf16[192,1280]{1,0:T(8,128)(2,1)S(1)} %get-tuple-element.43), channel_id=1, source_target_pairs={{0,1},{1,2},{2,3},{3,0},{4,5},{5,6},{6,7},{7,4},{8,9},{9,10},{10,1... | collective-permute-start | bytes 1474568 | tf_op jit(solution)/shard_map/ppermute | solution.py:338
  109.1 2.5 %collective-permute-start.15 = (bf16[192,1280]{1,0:T(8,128)(2,1)S(1)}, bf16[192,1280]{1,0:T(8,128)(2,1)}, u32[]{:S(2)}, u32[]{:S(2)}) collective-permute-start(bf16[192,1280]{1,0:T(8,128)(2,1)S(1)} %get-tuple-element.42), channel_id=1, source_target_pairs={{0,2},{1,3},{2,0},{3,1},{4,6},{5,7},{6,4},{7,5},{8,10},{9,11},{10,... | collective-permute-start | bytes 1474568 | tf_op jit(solution)/shard_map/ppermute | solution.py:338
  111.6 2.5 %collective-permute-start.14 = (bf16[192,1280]{1,0:T(8,128)(2,1)S(1)}, bf16[192,1280]{1,0:T(8,128)(2,1)}, u32[]{:S(2)}, u32[]{:S(2)}) collective-permute-start(bf16[192,1280]{1,0:T(8,128)(2,1)S(1)} %get-tuple-element.41), channel_id=1, source_target_pairs={{0,3},{1,0},{2,1},{3,2},{4,7},{5,4},{6,5},{7,6},{8,11},{9,8},{10,9... | collective-permute-start | bytes 1474568 | tf_op jit(solution)/shard_map/ppermute | solution.py:338
  114.1 11.5 %all-to-all-done.2 = bf16[32,24,384]{2,1,0:T(8,128)(2,1)S(1)} async-done(((bf16[32,24,384]{2,1,0:T(8,128)(2,1)}), bf16[32,24,384]{2,1,0:T(8,128)(2,1)S(1)}, u32[]{:S(2)}, u32[]{:S(2)}) %all-to-all-start.2) | async-done | bytes 589856 | tf_op jit(solution)/shard_map/all_to_all | solution.py:393
  125.8 3.0 %collective-permute-start.19 = (f32[20,320]{1,0:T(8,128)S(1)}, f32[20,320]{1,0:T(8,128)S(1)}, u32[]{:S(2)}, u32[]{:S(2)}) collective-permute-start(f32[20,320]{1,0:T(8,128)S(1)} %get-tuple-element.47), channel_id=1, source_target_pairs={{0,3},{1,0},{2,1},{3,2},{4,7},{5,4},{6,5},{7,6},{8,11},{9,8},{10,9... | collective-permute-start | bytes 76808 | tf_op jit(solution)/shard_map/ppermute | solution.py:338
  128.8 2.2 %collective-permute-start.18 = (f32[20,320]{1,0:T(8,128)S(1)}, f32[20,320]{1,0:T(8,128)S(1)}, u32[]{:S(2)}, u32[]{:S(2)}) collective-permute-start(f32[20,320]{1,0:T(8,128)S(1)} %get-tuple-element.47), channel_id=1, source_target_pairs={{0,2},{1,3},{2,0},{3,1},{4,6},{5,7},{6,4},{7,5},{8,10},{9,11},{10,... | collective-permute-start | bytes 76808 | tf_op jit(solution)/shard_map/ppermute | solution.py:338
  131.0 2.5 %collective-permute-start.17 = (f32[20,320]{1,0:T(8,128)S(1)}, f32[20,320]{1,0:T(8,128)S(1)}, u32[]{:S(2)}, u32[]{:S(2)}) collective-permute-start(f32[20,320]{1,0:T(8,128)S(1)} %get-tuple-element.47), channel_id=1, source_target_pairs={{0,1},{1,2},{2,3},{3,0},{4,5},{5,6},{6,7},{7,4},{8,9},{9,10},{10,1... | collective-permute-start | bytes 76808 | tf_op jit(solution)/shard_map/ppermute | solution.py:338
  134.4 2.3 %add_add_fusion = f32[192,1280]{1,0:T(8,128)} fusion(f32[192,1280]{1,0:T(8,128)S(1)} %get-tuple-element.36, bf16[192,1280]{1,0:T(8,128)(2,1)S(1)} %collective-permute-done.16, bf16[192,1280]{1,0:T(8,128)(2,1)} %collective-permute-done.15, bf16[192,1280]{1,0:T(8,128)(2,1)} %collective-permute-done.14), kind=kLoop, calls=%fused_computation.3 | loop fusion | flops 1474560 | bytes 3440640 | tf_op jit(solution)/shard_map/add | solution.py:400
  (77 shorter events, 17.3 us)
Async XLA Ops:
  16.0 28.0 %copy-start = (bf16[192,1280]{1,0:T(8,128)(2,1)S(1)}, bf16[192,1280]{1,0:T(8,128)(2,1)}, u32[]{:S(2)}) copy-start(bf16[192,1280]{1,0:T(8,128)(2,1)} %q_ref.3) | copy-start | bytes 1474564
  16.0 28.0 %copy-start.1 = (bf16[192,1280]{1,0:T(8,128)(2,1)S(1)}, bf16[192,1280]{1,0:T(8,128)(2,1)}, u32[]{:S(2)}) copy-start(bf16[192,1280]{1,0:T(8,128)(2,1)} %k_ref.3) | copy-start | bytes 1474564
  16.0 28.0 %copy-start.2 = (bf16[192,1280]{1,0:T(8,128)(2,1)S(1)}, bf16[192,1280]{1,0:T(8,128)(2,1)}, u32[]{:S(2)}) copy-start(bf16[192,1280]{1,0:T(8,128)(2,1)} %v_ref.2) | copy-start | bytes 1474564
  16.0 28.0 %copy-start.5 = (s32[1,192]{1,0:T(1,128)S(1)}, s32[1,192]{1,0:T(1,128)}, u32[]{:S(2)}) copy-start(s32[1,192]{1,0:T(1,128)} %ids_ref.3) | copy-start | bytes 2308
  16.0 30.5 %all-to-all-start = ((bf16[4,400,640]{2,1,0:T(8,128)(2,1)}), bf16[4,400,640]{2,1,0:T(8,128)(2,1)S(1)}, u32[]{:S(2)}, u32[]{:S(2)}) async-start(bf16[4,400,640]{2,1,0:T(8,128)(2,1)} %get-tuple-element.24), calls=%async_computation | async-start | bytes 4096000 | tf_op jit(solution)/shard_map/all_to_all | solution.py:367
  22.0 10.9 %collective-permute-start = (bf16[24,384]{1,0:T(8,128)(2,1)S(1)}, bf16[24,384]{1,0:T(8,128)(2,1)S(1)}, u32[]{:S(2)}, u32[]{:S(2)}) collective-permute-start(bf16[24,384]{1,0:T(8,128)(2,1)S(1)} %copy-done.12), channel_id=1, source_target_pairs={{0,64},{32,96},{64,128},{96,160},{128,192},{160,224},{192,0},{224,... | collective-permute-start | bytes 55304 | tf_op jit(solution)/shard_map/ppermute | solution.py:338
  24.2 8.7 %collective-permute-start.1 = (bf16[24,384]{1,0:T(8,128)(2,1)S(1)}, bf16[24,384]{1,0:T(8,128)(2,1)S(1)}, u32[]{:S(2)}, u32[]{:S(2)}) collective-permute-start(bf16[24,384]{1,0:T(8,128)(2,1)S(1)} %copy-done.12), channel_id=1, source_target_pairs={{0,128},{32,160},{64,192},{96,224},{128,0},{160,32},{192,64},{224,... | collective-permute-start | bytes 55304 | tf_op jit(solution)/shard_map/ppermute | solution.py:338
  29.6 4.7 %collective-permute-start.2 = (bf16[24,384]{1,0:T(8,128)(2,1)S(1)}, bf16[24,384]{1,0:T(8,128)(2,1)S(1)}, u32[]{:S(2)}, u32[]{:S(2)}) collective-permute-start(bf16[24,384]{1,0:T(8,128)(2,1)S(1)} %copy-done.12), channel_id=1, source_target_pairs={{0,192},{32,224},{64,0},{96,32},{128,64},{160,96},{192,128},{224,1... | collective-permute-start | bytes 55304 | tf_op jit(solution)/shard_map/ppermute | solution.py:338
  34.3 5.8 %collective-permute-start.3 = (bf16[96,384]{1,0:T(8,128)(2,1)S(1)}, bf16[96,384]{1,0:T(8,128)(2,1)S(1)}, u32[]{:S(2)}, u32[]{:S(2)}) collective-permute-start(bf16[96,384]{1,0:T(8,128)(2,1)S(1)} %pad_maximum_fusion.1), channel_id=1, source_target_pairs={{0,32},{32,64},{64,96},{96,128},{128,160},{160,192},{192,224},{224... | collective-permute-start | bytes 221192 | tf_op jit(solution)/shard_map/ppermute | solution.py:338
  40.8 8.7 %collective-permute-start.4 = (bf16[192,384]{1,0:T(8,128)(2,1)}, bf16[192,384]{1,0:T(8,128)(2,1)}, u32[]{:S(2)}, u32[]{:S(2)}) collective-permute-start(bf16[192,384]{1,0:T(8,128)(2,1)} %constant_dynamic-update-slice_fusion), channel_id=1, source_target_pairs={{0,8},{8,16},{16,24},{24,0},{1,9},{9,17},{17,25},{25,1},{2,10},{10... | collective-permute-start | bytes 442376 | tf_op jit(solution)/shard_map/ppermute | solution.py:338
  42.3 7.1 %collective-permute-start.5 = (bf16[192,384]{1,0:T(8,128)(2,1)}, bf16[192,384]{1,0:T(8,128)(2,1)}, u32[]{:S(2)}, u32[]{:S(2)}) collective-permute-start(bf16[192,384]{1,0:T(8,128)(2,1)} %constant_dynamic-update-slice_fusion), channel_id=1, source_target_pairs={{0,24},{8,0},{16,8},{24,16},{1,25},{9,1},{17,9},{25,17},{2,26},{10... | collective-permute-start | bytes 442376 | tf_op jit(solution)/shard_map/ppermute | solution.py:338
  49.5 11.0 %copy-start.4 = (bf16[192,1280]{1,0:T(8,128)(2,1)S(1)}, bf16[192,1280]{1,0:T(8,128)(2,1)}, u32[]{:S(2)}) copy-start(bf16[192,1280]{1,0:T(8,128)(2,1)} %copy-done.3) | copy-start | bytes 1474564
  49.5 42.7 %all-to-all-start.1 = ((bf16[64,24,384]{2,1,0:T(8,128)(2,1)}), bf16[64,24,384]{2,1,0:T(8,128)(2,1)S(1)}, u32[]{:S(2)}, u32[]{:S(2)}) async-start(bf16[64,24,384]{2,1,0:T(8,128)(2,1)} %bitcast.2), calls=%async_computation.1 | async-start | bytes 2359296 | tf_op jit(solution)/shard_map/all_to_all | solution.py:377
  60.5 13.3 %collective-permute-start.6 = (bf16[192,1280]{1,0:T(8,128)(2,1)S(1)}, bf16[192,1280]{1,0:T(8,128)(2,1)S(1)}, u32[]{:S(2)}, u32[]{:S(2)}) collective-permute-start(bf16[192,1280]{1,0:T(8,128)(2,1)S(1)} %copy-done.4), channel_id=1, source_target_pairs={{0,1},{1,2},{2,3},{3,0},{4,5},{5,6},{6,7},{7,4},{8,9},{9,10},{10,1... | collective-permute-start | bytes 1474568 | tf_op jit(solution)/shard_map/ppermute | solution.py:338
  60.6 13.6 %collective-permute-start.8 = (bf16[192,1280]{1,0:T(8,128)(2,1)S(1)}, bf16[192,1280]{1,0:T(8,128)(2,1)S(1)}, u32[]{:S(2)}, u32[]{:S(2)}) collective-permute-start(bf16[192,1280]{1,0:T(8,128)(2,1)S(1)} %copy-done.4), channel_id=1, source_target_pairs={{0,3},{1,0},{2,1},{3,2},{4,7},{5,4},{6,5},{7,6},{8,11},{9,8},{10,9... | collective-permute-start | bytes 1474568 | tf_op jit(solution)/shard_map/ppermute | solution.py:338
  63.5 6.7 %collective-permute-start.10 = (bf16[96,384]{1,0:T(8,128)(2,1)S(1)}, bf16[96,384]{1,0:T(8,128)(2,1)S(1)}, u32[]{:S(2)}, u32[]{:S(2)}) collective-permute-start(bf16[96,384]{1,0:T(8,128)(2,1)S(1)} %slice.17), channel_id=1, source_target_pairs={{0,8},{8,16},{16,24},{24,0},{1,9},{9,17},{17,25},{25,1},{2,10},{10... | collective-permute-start | bytes 221192 | tf_op jit(solution)/shard_map/ppermute | solution.py:338
  66.0 4.7 %collective-permute-start.11 = (bf16[96,384]{1,0:T(8,128)(2,1)S(1)}, bf16[96,384]{1,0:T(8,128)(2,1)S(1)}, u32[]{:S(2)}, u32[]{:S(2)}) collective-permute-start(bf16[96,384]{1,0:T(8,128)(2,1)S(1)} %slice.18), channel_id=1, source_target_pairs={{0,24},{8,0},{16,8},{24,16},{1,25},{9,1},{17,9},{25,17},{2,26},{10... | collective-permute-start | bytes 221192 | tf_op jit(solution)/shard_map/ppermute | solution.py:338
  71.6 10.4 %copy-start.13 = (bf16[768,384]{1,0:T(8,128)(2,1)}, bf16[768,384]{1,0:T(8,128)(2,1)S(1)}, u32[]{:S(2)}) copy-start(bf16[768,384]{1,0:T(8,128)(2,1)S(1)} %constant_dynamic-update-slice_fusion.5.near_ref) | copy-start | bytes 1769476
  71.6 6.0 %collective-permute-start.12 = (bf16[768,384]{1,0:T(8,128)(2,1)S(1)}, bf16[768,384]{1,0:T(8,128)(2,1)}, u32[]{:S(2)}, u32[]{:S(2)}) collective-permute-start(bf16[768,384]{1,0:T(8,128)(2,1)S(1)} %constant_dynamic-update-slice_fusion.5.near_ref), channel_id=1, source_target_pairs={{0,4},{4,0},{1,5},{5,1},{2,6},{6,2},{3,7},{7,3},{8,12},{12,8},{9,1... | collective-permute-start | bytes 1769480 | tf_op jit(solution)/shard_map/ppermute | solution.py:338
  73.8 8.2 %copy-start.10 = (bf16[192,1280]{1,0:T(8,128)(2,1)}, bf16[192,1280]{1,0:T(8,128)(2,1)S(1)}, u32[]{:S(2)}) copy-start(bf16[192,1280]{1,0:T(8,128)(2,1)S(1)} %collective-permute-done.6.c1_ref) | copy-start | bytes 1474564
  73.8 8.2 %collective-permute-start.7 = (bf16[96,1280]{1,0:T(8,128)(2,1)S(1)}, bf16[96,1280]{1,0:T(8,128)(2,1)}, u32[]{:S(2)}, u32[]{:S(2)}) collective-permute-start(bf16[96,1280]{1,0:T(8,128)(2,1)S(1)} %slice.22), channel_id=1, source_target_pairs={{0,1},{1,2},{2,3},{3,0},{4,5},{5,6},{6,7},{7,4},{8,9},{9,10},{10,1... | collective-permute-start | bytes 737288 | tf_op jit(solution)/shard_map/ppermute | solution.py:338
  74.1 7.8 %copy-start.11 = (bf16[192,1280]{1,0:T(8,128)(2,1)}, bf16[192,1280]{1,0:T(8,128)(2,1)S(1)}, u32[]{:S(2)}) copy-start(bf16[192,1280]{1,0:T(8,128)(2,1)S(1)} %collective-permute-done.8.c4_ref) | copy-start | bytes 1474564
  74.2 7.8 %collective-permute-start.9 = (bf16[96,1280]{1,0:T(8,128)(2,1)S(1)}, bf16[96,1280]{1,0:T(8,128)(2,1)}, u32[]{:S(2)}, u32[]{:S(2)}) collective-permute-start(bf16[96,1280]{1,0:T(8,128)(2,1)S(1)} %slice.23), channel_id=1, source_target_pairs={{0,3},{1,0},{2,1},{3,2},{4,7},{5,4},{6,5},{7,6},{8,11},{9,8},{10,9... | collective-permute-start | bytes 737288 | tf_op jit(solution)/shard_map/ppermute | solution.py:338
  77.6 14.6 %copy-start.6 = (s32[1,1536]{1,0:T(1,128)S(1)}, s32[1,1536]{1,0:T(1,128)}, u32[]{:S(2)}) copy-start(s32[1,1536]{1,0:T(1,128)} %constant.42.clone.t_ref) | copy-start | bytes 18436
  98.3 2.1 %collective-permute-start.13 = (bf16[768,384]{1,0:T(8,128)(2,1)S(1)}, bf16[768,384]{1,0:T(8,128)(2,1)S(1)}, u32[]{:S(2)}, u32[]{:S(2)}) collective-permute-start(bf16[768,384]{1,0:T(8,128)(2,1)S(1)} %get-tuple-element.37), channel_id=1, source_target_pairs={{0,4},{4,0},{1,5},{5,1},{2,6},{6,2},{3,7},{7,3},{8,12},{12,8},{9,1... | collective-permute-start | bytes 1769480 | tf_op jit(solution)/shard_map/ppermute | solution.py:338
  101.3 24.4 %all-to-all-start.2 = ((bf16[32,24,384]{2,1,0:T(8,128)(2,1)}), bf16[32,24,384]{2,1,0:T(8,128)(2,1)S(1)}, u32[]{:S(2)}, u32[]{:S(2)}) async-start(bf16[32,24,384]{2,1,0:T(8,128)(2,1)} %bitcast.17), calls=%async_computation.2 | async-start | bytes 1179648 | tf_op jit(solution)/shard_map/all_to_all | solution.py:393
  106.3 24.7 %collective-permute-start.16 = (bf16[192,1280]{1,0:T(8,128)(2,1)S(1)}, bf16[192,1280]{1,0:T(8,128)(2,1)S(1)}, u32[]{:S(2)}, u32[]{:S(2)}) collective-permute-start(bf16[192,1280]{1,0:T(8,128)(2,1)S(1)} %get-tuple-element.43), channel_id=1, source_target_pairs={{0,1},{1,2},{2,3},{3,0},{4,5},{5,6},{6,7},{7,4},{8,9},{9,10},{10,1... | collective-permute-start | bytes 1474568 | tf_op jit(solution)/shard_map/ppermute | solution.py:338
  109.1 24.5 %collective-permute-start.15 = (bf16[192,1280]{1,0:T(8,128)(2,1)S(1)}, bf16[192,1280]{1,0:T(8,128)(2,1)}, u32[]{:S(2)}, u32[]{:S(2)}) collective-permute-start(bf16[192,1280]{1,0:T(8,128)(2,1)S(1)} %get-tuple-element.42), channel_id=1, source_target_pairs={{0,2},{1,3},{2,0},{3,1},{4,6},{5,7},{6,4},{7,5},{8,10},{9,11},{10,... | collective-permute-start | bytes 1474568 | tf_op jit(solution)/shard_map/ppermute | solution.py:338
  111.6 22.9 %collective-permute-start.14 = (bf16[192,1280]{1,0:T(8,128)(2,1)S(1)}, bf16[192,1280]{1,0:T(8,128)(2,1)}, u32[]{:S(2)}, u32[]{:S(2)}) collective-permute-start(bf16[192,1280]{1,0:T(8,128)(2,1)S(1)} %get-tuple-element.41), channel_id=1, source_target_pairs={{0,3},{1,0},{2,1},{3,2},{4,7},{5,4},{6,5},{7,6},{8,11},{9,8},{10,9... | collective-permute-start | bytes 1474568 | tf_op jit(solution)/shard_map/ppermute | solution.py:338
  125.8 10.9 %collective-permute-start.19 = (f32[20,320]{1,0:T(8,128)S(1)}, f32[20,320]{1,0:T(8,128)S(1)}, u32[]{:S(2)}, u32[]{:S(2)}) collective-permute-start(f32[20,320]{1,0:T(8,128)S(1)} %get-tuple-element.47), channel_id=1, source_target_pairs={{0,3},{1,0},{2,1},{3,2},{4,7},{5,4},{6,5},{7,6},{8,11},{9,8},{10,9... | collective-permute-start | bytes 76808 | tf_op jit(solution)/shard_map/ppermute | solution.py:338
  128.8 7.9 %collective-permute-start.18 = (f32[20,320]{1,0:T(8,128)S(1)}, f32[20,320]{1,0:T(8,128)S(1)}, u32[]{:S(2)}, u32[]{:S(2)}) collective-permute-start(f32[20,320]{1,0:T(8,128)S(1)} %get-tuple-element.47), channel_id=1, source_target_pairs={{0,2},{1,3},{2,0},{3,1},{4,6},{5,7},{6,4},{7,5},{8,10},{9,11},{10,... | collective-permute-start | bytes 76808 | tf_op jit(solution)/shard_map/ppermute | solution.py:338
  131.0 5.7 %collective-permute-start.17 = (f32[20,320]{1,0:T(8,128)S(1)}, f32[20,320]{1,0:T(8,128)S(1)}, u32[]{:S(2)}, u32[]{:S(2)}) collective-permute-start(f32[20,320]{1,0:T(8,128)S(1)} %get-tuple-element.47), channel_id=1, source_target_pairs={{0,1},{1,2},{2,3},{3,0},{4,5},{5,6},{6,7},{7,4},{8,9},{9,10},{10,1... | collective-permute-start | bytes 76808 | tf_op jit(solution)/shard_map/ppermute | solution.py:338
  (5 other events, 13.0 us)
